TPU v7x, 32 devices: a whole 2x2x4 slice. The times are simulated.
32 devices in a mesh: grp: 4 (over y, x), slab: 8 (over z, core).
Axes of the slice: x: 2, y: 2, z: 4, core: 2. Of those that a mesh axis runs over, the one named last changes fastest.
Arguments:
- margin: bfloat16 [128, 5, 128, 128], P(('grp', 'slab')), may hold values from -2 to 2
- factor: bfloat16 [128, 5, 128, 128], P(('grp', 'slab')), may hold values from -2 to 2
- pattern: int32 [128, 5], P(('grp', 'slab')), may hold values from 0 to 1, as said below
Outputs:
- refined: bfloat16 [128, 5, 128, 128], P(('grp', 'slab'))
- defect_norm: float32 [], replicated
Inputs may be any that keep to these rules, and one draw needn't show every extreme that they name: The pattern is symmetric: pattern[j, o] equals pattern[j + o - 2, 4 - o]. The diagonal block (o = 2) is always present and blocks whose row lies outside the matrix are absent; the share of present blocks varies from region to region.
All inputs are finite; a program needn't handle non-finite values.
Results may differ from a plain program's by a relative error of at most 0.0054.
Values may be sent and summed in bfloat16 or wider, within the bound.
No kernel may reach another device: no remote copies, remote signals or barrier semaphores. Data moves between devices by JAX's collectives and lax.ppermute only.
A program may use at most 64 MiB of HBM per device.

v0:
```python
import functools

import jax
import jax.numpy as jnp
from jax import lax
from jax.experimental import pallas as pl
from jax.experimental.pallas import tpu as pltpu
from jax.sharding import PartitionSpec as P


AXES = ("grp", "slab")
HBM = pl.BlockSpec(memory_space=pltpu.HBM)
VMEM = pl.BlockSpec(memory_space=pltpu.VMEM)
SMEM = pl.BlockSpec(memory_space=pltpu.SMEM)
PARAMS = pltpu.CompilerParams(vmem_limit_bytes=32 * 1024 * 1024)
FLAG_ROWS = 16


class Sizes:
    def __init__(self, shape, quarter_len, devices):
        self.columns, self.offsets, self.block, _ = shape
        self.half = (self.offsets - 1) // 2
        self.tile = self.half * self.block
        self.cells = self.half * self.offsets
        self.flag_blocks = -(-self.half * self.half * FLAG_ROWS // self.block)
        self.quarter_len = quarter_len
        self.devices = devices
        self.entries = self.columns * devices * self.block

    def cost(self, products, moved):
        return pl.CostEstimate(
            flops=products * 2 * self.tile**3, bytes_accessed=moved * 2**20, transcendentals=0
        )

    def tiles(self, count, dtype):
        return jax.ShapeDtypeStruct((count, self.tile, self.tile), dtype)


def odd_device():
    return lax.rem(lax.axis_index("slab"), 2)


def half_starts(z):
    near = jnp.where(odd_device() == 1, 0, z.columns - z.half)
    return near, z.columns - z.half - near


def keep(flag, value):
    return jnp.where(flag, value, jnp.zeros_like(value))


def dot(left, right):
    return jnp.dot(left, right, preferred_element_type=jnp.float32)


def chain_tile(true_tile):
    return jnp.where(odd_device() == 1, 2 - true_tile, true_tile)


def expand(z, out, read):
    block = z.block
    for t in range(z.half):
        for a in range(3 * z.half):
            o = a - t
            u = a % z.half
            if 0 <= o < z.offsets:
                value = read(t, o)
            else:
                value = jnp.zeros((block, block), out.dtype)
            out[
                chain_tile(a // z.half),
                u * block : (u + 1) * block,
                t * block : (t + 1) * block,
            ] = value


def offset_of(z, e, t, u):
    return jnp.where(odd_device() == 1, 1 - e, e - 1) * z.half + u - t + z.half


def flag_of(z, pattern, first, e, t, u):
    o = offset_of(z, e, t, u)
    inside = jnp.logical_and(o >= 0, o < z.offsets)
    return jnp.logical_and(inside, pattern[first + t, jnp.clip(o, 0, z.offsets - 1)] != 0)


def masked(z, value, flag):
    block = z.block
    rows = []
    for u in range(z.half):
        rows.append(
            jnp.concatenate(
                [
                    keep(
                        flag(t, u),
                        value[u * block : (u + 1) * block, t * block : (t + 1) * block],
                    )
                    for t in range(z.half)
                ],
                axis=1,
            )
        )
    return jnp.concatenate(rows, axis=0)


def own_masked(z, pattern, first, e, value):
    return masked(z, value, lambda t, u: flag_of(z, pattern, first, e, t, u))


def identity(z):
    shape = (z.tile, z.tile)
    rows = lax.broadcasted_iota(jnp.int32, shape, 0)
    return (rows == lax.broadcasted_iota(jnp.int32, shape, 1)).astype(jnp.float32)


def tile_product(left, right, i, c, low, high):
    total = None
    for k in range(max(low, i - 1, c - 1), min(high, i + 1, c + 1) + 1):
        term = dot(left[k][i - k + 1], right[k - c + 1])
        total = term if total is None else total + term
    return total


def sum_squares(z, value):
    wide = value.astype(jnp.float32)
    return jnp.sum((wide * wide).reshape(-1, 8, z.tile), axis=0)


def store_half(z, tiles, cells):
    block = z.block
    for t in range(z.half):
        for o in range(z.offsets):
            a = t + o
            u = a % z.half
            value = tiles[
                chain_tile(a // z.half),
                u * block : (u + 1) * block,
                t * block : (t + 1) * block,
            ]
            cells[t, o] = value.astype(cells.dtype)


def mask_kernel(z, pattern, mask_near):
    first, _ = half_starts(z)
    ones = jnp.ones((z.tile, z.tile), jnp.float32)
    for e in range(3):
        mask_near[e] = own_masked(z, pattern, first, e, ones).astype(mask_near.dtype)


def masks(z, pattern, kind):
    return pl.pallas_call(
        functools.partial(mask_kernel, z),
        out_shape=z.tiles(3, kind),
        in_specs=[SMEM],
        out_specs=VMEM,
        compiler_params=PARAMS,
        cost_estimate=z.cost(20, 1),
        name="masks",
    )(pattern)


def pack_kernel(z, margin, factor, pattern, _, near, far, cross):
    near_first, far_first = half_starts(z)
    first_row = lax.axis_index("slab") * z.columns
    plan = ((margin, far_first), (factor, far_first), (margin, near_first), (factor, near_first))
    for k, (source, first) in enumerate(plan):
        for t in range(z.half):
            for o in range(z.offsets):
                flag = pattern[first + t, o] != 0
                if k % 2:
                    row = first_row + first + t + o - z.half
                    inside = jnp.logical_and(row >= 0, row < z.quarter_len)
                    flag = jnp.logical_and(flag, inside)
                value = keep(flag, source[first + t, o])
                cell = t * z.offsets + o
                u = o + t - z.half
                if k == 0:
                    far[cell] = value
                    near[2 * z.cells + cell] = value
                elif k == 1:
                    far[z.cells + cell] = value
                    if 0 <= u < z.half:
                        cross[t, u] = value
                else:
                    near[(k - 2) * z.cells + cell] = value
    per_block = z.block // FLAG_ROWS
    for f in range(z.flag_blocks * per_block):
        t, u = f // z.half, f % z.half
        value = jnp.zeros((FLAG_ROWS, z.block), near.dtype)
        if t < z.half:
            value = keep(pattern[near_first + t, u - t + z.half] != 0, jnp.ones_like(value))
        low = f % per_block * FLAG_ROWS
        near[3 * z.cells + f // per_block, low : low + FLAG_ROWS] = value


def pack(z, margin, factor, pattern, mask_near):
    kind = margin.dtype
    return pl.pallas_call(
        functools.partial(pack_kernel, z),
        out_shape=(
            jax.ShapeDtypeStruct((3 * z.cells + z.flag_blocks, z.block, z.block), kind),
            jax.ShapeDtypeStruct((2 * z.cells, z.block, z.block), kind),
            jax.ShapeDtypeStruct((z.half, z.half, z.block, z.block), kind),
        ),
        in_specs=[VMEM, VMEM, SMEM, VMEM],
        out_specs=(VMEM, VMEM, VMEM),
        compiler_params=PARAMS,
        name="pack",
    )(margin, factor, pattern, mask_near)


def inner_kernel(
    z, pattern, mask_near, near, far, beside, z_cols, turned, p_part, d_part, squares, held16, held32,
    s_cols, z_turned, image, d_near, d_beside, sums, sems,
):
    near_first, _ = half_starts(z)
    kind = near.dtype

    def cells_of(ref, base):
        return lambda t, o: ref[base + t * z.offsets + o]

    expand(z, s_cols.at[0], cells_of(far, 0))
    expand(z, s_cols.at[1], cells_of(near, 0))
    expand(z, s_cols.at[2], cells_of(beside, 0))
    expand(z, s_cols.at[3], cells_of(beside, 2 * z.cells))
    expand(z, z_cols.at[0], cells_of(far, z.cells))
    expand(z, z_cols.at[1], cells_of(near, z.cells))
    expand(z, z_cols.at[2], cells_of(beside, z.cells))
    moves = [
        (z_cols.at[0], held16.at[pl.ds(2, 3)]),
        (z_cols.at[1], held16.at[pl.ds(5, 3)]),
        (z_cols.at[2, pl.ds(0, 2)], held16.at[pl.ds(8, 2)]),
        (d_near.at[pl.ds(0, 2)], held16.at[pl.ds(0, 2)]),
        (sums, held32),
    ]
    copies = [
        pltpu.make_async_copy(source, target, sems.at[k]) for k, (source, target) in enumerate(moves)
    ]
    for copy in copies[:3]:
        copy.start()
    for x in range(3):
        for e in range(3):
            z_turned[x, e] = z_cols[x, e].T
    turned[0] = z_turned[0, 0]
    turned[1] = z_turned[0, 1]
    turned[2] = z_turned[1, 0]

    def image_tile(y, c):
        total = None
        for inner in range(max(c - 1, y - 1, 1), min(c + 1, y + 1) + 1):
            term = dot(s_cols[inner - 1, y - inner + 1], z_cols[c - 1, inner - c + 1])
            total = term if total is None else total + term
        return total

    def turned_sum(i, c, rows):
        total = None
        for m in rows:
            term = dot(z_turned[i - 1, m - i + 1], image[c - 1, m])
            total = term if total is None else total + term
        return total

    p_part[0] = image_tile(0, 1)
    p_part[1] = image_tile(1, 1)
    for c, rows in ((1, (2, 3)), (2, (0, 1, 2, 3, 4)), (3, (1, 2, 3, 4))):
        for y in rows:
            image[c - 1, y] = image_tile(y, c).astype(kind)
    d_part[0] = turned_sum(1, 1, (2,))
    d_part[1] = turned_sum(2, 1, (2, 3))
    eye = identity(z)
    total = jnp.zeros((8, z.tile), jnp.float32)
    for i in (1, 2, 3):
        value = -turned_sum(i, 2, (i - 1, i, i + 1))
        if i == 2:
            value = eye + value
        value = (value * mask_near[i - 1].astype(jnp.float32)).astype(kind)
        d_near[i - 1] = value
        total = total + sum_squares(z, value)
    squares[...] = total
    copies[3].start()

    def side_flag(t, u):
        o = offset_of(z, 0, t, u)
        inside = jnp.logical_and(o >= 0, o < z.offsets)
        back = jnp.clip(z.offsets - 1 - o, 0, z.offsets - 1)
        return jnp.logical_and(inside, pattern[near_first + u, back] != 0)

    d_beside[0] = masked(z, -turned_sum(2, 3, (1, 2, 3)), side_flag).astype(kind)
    value = eye - turned_sum(3, 3, (2, 3, 4))
    block = z.block
    per_block = block // FLAG_ROWS
    for t in range(z.half):
        for u in range(z.half):
            f = t * z.half + u
            low = f % per_block * FLAG_ROWS
            flags = beside[3 * z.cells + f // per_block, low : low + FLAG_ROWS]
            flag = flags.astype(jnp.float32)[:1]
            part = (slice(u * block, (u + 1) * block), slice(t * block, (t + 1) * block))
            d_beside[1, part[0], part[1]] = (value[part] * flag).astype(kind)

    factor = (None, z_cols.at[0], z_cols.at[1], z_cols.at[2])
    defect = (None, None, d_near, d_beside)
    for i in (1, 2, 3):
        sums[i - 1] = z_cols[1, i - 1].astype(jnp.float32) + 0.5 * tile_product(
            factor, d_near, i, 2, 1, 3
        )
        sums[2 + i] = tile_product(defect, d_near, i, 2, 2, 3)
    copies[4].start()
    for copy in copies:
        copy.wait()


def inner_step(z, pattern, mask_near, near, far, beside):
    kind = near.dtype
    tile = z.tile
    return pl.pallas_call(
        functools.partial(inner_kernel, z),
        out_shape=(
            jax.ShapeDtypeStruct((3, 3, tile, tile), kind),
            z.tiles(3, kind),
            z.tiles(2, jnp.float32),
            z.tiles(2, jnp.float32),
            jax.ShapeDtypeStruct((8, tile), jnp.float32),
            z.tiles(10, kind),
            z.tiles(6, jnp.float32),
        ),
        in_specs=[SMEM, VMEM, VMEM, VMEM, VMEM],
        out_specs=(VMEM,) * 5 + (HBM,) * 2,
        scratch_shapes=[
            pltpu.VMEM((4, 3, tile, tile), kind),
            pltpu.VMEM((3, 3, tile, tile), kind),
            pltpu.VMEM((3, 5, tile, tile), kind),
            pltpu.VMEM((3, tile, tile), kind),
            pltpu.VMEM((2, tile, tile), kind),
            pltpu.VMEM((6, tile, tile), jnp.float32),
            pltpu.SemaphoreType.DMA((5,)),
        ],
        compiler_params=PARAMS,
        cost_estimate=z.cost(54, 8),
        name="inner",
    )(pattern, mask_near, near, far, beside)


def outer_kernel(
    z, pattern, far, cross, z_cols, turned, p_part, d_part, squares, d_out, carry, spread, s_far, z_far,
    d_far, sems,
):
    _, far_first = half_starts(z)
    kind = far.dtype

    def factor_cell(t, o):
        value = far[z.cells + t * z.offsets + o]
        u = o + t - z.half
        if 0 <= u < z.half:
            value = value + cross[t, u]
        return value

    expand(z, s_far, lambda t, o: far[t * z.offsets + o])
    expand(z, z_far, factor_cell)
    copies = [pltpu.make_async_copy(z_far.at[pl.ds(1, 2)], carry.at[pl.ds(0, 2)], sems.at[0])]
    copies[0].start()
    link = z_cols[0, 0]
    image = (
        dot(s_far[0], link).astype(kind),
        (dot(s_far[1], link) + p_part[0]).astype(kind),
        (dot(s_far[2], link) + p_part[1]).astype(kind),
    )
    values = (
        -(dot(z_far[0].T, image[0]) + dot(z_far[1].T, image[1]) + dot(z_far[2].T, image[2])),
        identity(z) - (dot(turned[0], image[1]) + dot(turned[1], image[2]) + d_part[0]),
        -(dot(turned[2], image[2]) + d_part[1]),
    )
    total = squares[...]
    for e, value in enumerate(values):
        value = own_masked(z, pattern, far_first, e, value).astype(kind)
        d_far[e] = value
        copies.append(
            pltpu.make_async_copy(d_far.at[pl.ds(e, 1)], carry.at[pl.ds(2 + e, 1)], sems.at[1 + e])
        )
        copies[-1].start()
        if e < 2:
            d_out[e] = value
        total = total + sum_squares(z, value)
    lanes = jnp.sum(total, axis=0, keepdims=True)
    folded = lanes[:, : z.block]
    for t in range(1, z.half):
        folded = folded + lanes[:, t * z.block : (t + 1) * z.block]
    spread[...] = jnp.broadcast_to(folded[None], spread.shape)
    for copy in copies:
        copy.wait()


def outer_step(z, pattern, far, cross, z_cols, turned, p_part, d_part, squares):
    kind = far.dtype
    return pl.pallas_call(
        functools.partial(outer_kernel, z),
        out_shape=(
            z.tiles(2, kind),
            z.tiles(5, kind),
            jax.ShapeDtypeStruct((z.devices, 1, z.block), jnp.float32),
        ),
        in_specs=[SMEM] + [VMEM] * 7,
        out_specs=(VMEM, HBM, VMEM),
        scratch_shapes=[
            pltpu.VMEM((3, z.tile, z.tile), kind),
            pltpu.VMEM((3, z.tile, z.tile), kind),
            pltpu.VMEM((3, z.tile, z.tile), kind),
            pltpu.SemaphoreType.DMA((4,)),
        ],
        compiler_params=PARAMS,
        cost_estimate=z.cost(9, 4),
        name="outer",
    )(pattern, far, cross, z_cols, turned, p_part, d_part, squares)


def middle_kernel(
    z, pattern_in, held16_in, held32_in, carry_in, refined, _a, _b, _c, pattern, held16, held32, d_far,
    square, tiles, cells, sems,
):
    first, _ = half_starts(z)
    moves = (
        (pattern_in, pattern),
        (carry_in.at[pl.ds(3, 2)], d_far),
        (held16_in.at[pl.ds(0, 1)], held16.at[pl.ds(0, 1)]),
        (held32_in.at[pl.ds(3, 3)], held32.at[pl.ds(3, 3)]),
        (held16_in.at[pl.ds(3, 7)], held16.at[pl.ds(3, 7)]),
        (held32_in.at[pl.ds(0, 3)], held32.at[pl.ds(0, 3)]),
    )
    copies = [
        pltpu.make_async_copy(source, target, sems.at[k]) for k, (source, target) in enumerate(moves)
    ]
    for copy in copies:
        copy.start()
    for copy in copies[:4]:
        copy.wait()
    for i in (1, 2, 3):
        value = held32[2 + i]
        if i < 3:
            value = value + dot(d_far[i - 1], held16[0])
        square[i - 1] = own_masked(z, pattern, first, i - 1, value).astype(square.dtype)
    for copy in copies[4:]:
        copy.wait()
    for i in (1, 2, 3):
        total = None
        for k in range(max(1, i - 1), min(3, i + 1) + 1):
            term = dot(held16[3 * k - 1 + i - k + 1], square[k - 1])
            total = term if total is None else total + term
        tiles[i - 1] = own_masked(z, pattern, first, i - 1, held32[i - 1] + 0.375 * total)
    store_half(z, tiles, cells)
    copy = pltpu.make_async_copy(cells, refined.at[pl.ds(first, z.half)], sems.at[6])
    copy.start()
    copy.wait()


def middle_step(z, pattern, held16, held32, carry):
    kind = held16.dtype
    shape = (z.columns, z.offsets, z.block, z.block)
    return pl.pallas_call(
        functools.partial(middle_kernel, z),
        out_shape=(
            jax.ShapeDtypeStruct(shape, kind),
            jax.ShapeDtypeStruct(held16.shape, kind),
            jax.ShapeDtypeStruct(held32.shape, jnp.float32),
            jax.ShapeDtypeStruct(carry.shape, kind),
        ),
        in_specs=[HBM] * 4,
        out_specs=(HBM,) * 4,
        scratch_shapes=[
            pltpu.SMEM(pattern.shape, pattern.dtype),
            pltpu.VMEM(held16.shape, kind),
            pltpu.VMEM(held32.shape, jnp.float32),
            pltpu.VMEM((2, z.tile, z.tile), kind),
            pltpu.VMEM((3, z.tile, z.tile), kind),
            pltpu.VMEM((3, z.tile, z.tile), jnp.float32),
            pltpu.VMEM((z.half,) + shape[1:], kind),
            pltpu.SemaphoreType.DMA((7,)),
        ],
        input_output_aliases={1: 1, 2: 2, 3: 3},
        compiler_params=PARAMS,
        cost_estimate=z.cost(9, 6),
        name="middle",
    )(pattern, held16, held32, carry)


def last_kernel(
    z, pattern_in, held16, carry, d_in, _, refined, _a, _b, _c, pattern, narrow, d_beyond, square, tiles,
    cells, sems,
):
    _, first = half_starts(z)
    moves = (
        (pattern_in, pattern),
        (d_in, d_beyond),
        (carry.at[pl.ds(2, 3)], narrow.at[pl.ds(0, 3)]),
        (held16.at[pl.ds(0, 2)], narrow.at[pl.ds(3, 2)]),
        (carry.at[pl.ds(0, 2)], narrow.at[pl.ds(5, 2)]),
        (held16.at[pl.ds(2, 5)], narrow.at[pl.ds(7, 5)]),
    )
    copies = [
        pltpu.make_async_copy(source, target, sems.at[k]) for k, (source, target) in enumerate(moves)
    ]
    for copy in copies:
        copy.start()
    for copy in copies[:4]:
        copy.wait()
    values = (
        dot(d_beyond[1], narrow[0]) + dot(narrow[0], narrow[1]),
        dot(d_beyond[0], narrow[0]) + dot(narrow[1], narrow[1]) + dot(narrow[3], narrow[2]),
        dot(narrow[2], narrow[1]) + dot(narrow[4], narrow[2]),
    )
    for i, value in enumerate(values):
        square[i] = own_masked(z, pattern, first, i, value).astype(square.dtype)
    for copy in copies[4:]:
        copy.wait()
    base = (4, 7, 10)
    for i in (0, 1, 2):
        half = None
        rest = None
        for k in range(max(0, i - 1), min(2, i + 1) + 1):
            left = narrow[base[k] + i - k + 1]
            term = dot(left, narrow[k])
            half = term if half is None else half + term
            term = dot(left, square[k])
            rest = term if rest is None else rest + term
        value = narrow[7 + i].astype(jnp.float32) + 0.5 * half + 0.375 * rest
        tiles[i] = own_masked(z, pattern, first, i, value)
    store_half(z, tiles, cells)
    copy = pltpu.make_async_copy(cells, refined.at[pl.ds(first, z.half)], sems.at[6])
    copy.start()
    copy.wait()


def last_step(z, pattern, held16, carry, d_in, refined):
    kind = refined.dtype
    return pl.pallas_call(
        functools.partial(last_kernel, z),
        out_shape=tuple(
            jax.ShapeDtypeStruct(held.shape, held.dtype) for held in (refined, held16, carry, d_in)
        ),
        in_specs=[HBM] * 5,
        out_specs=(HBM,) * 4,
        scratch_shapes=[
            pltpu.SMEM(pattern.shape, pattern.dtype),
            pltpu.VMEM((12, z.tile, z.tile), kind),
            pltpu.VMEM(d_in.shape, kind),
            pltpu.VMEM((3, z.tile, z.tile), kind),
            pltpu.VMEM((3, z.tile, z.tile), jnp.float32),
            pltpu.VMEM((z.half,) + refined.shape[1:], kind),
            pltpu.SemaphoreType.DMA((7,)),
        ],
        input_output_aliases={4: 0, 1: 1, 2: 2, 3: 3},
        compiler_params=PARAMS,
        cost_estimate=z.cost(21, 4),
        name="last",
    )(pattern, held16, carry, d_in, refined)


def norm_kernel(z, gathered, _, norm):
    mean = jnp.sum(gathered[...]) * (1.0 / z.entries)
    norm[...] = jnp.sqrt(jnp.full(norm.shape, mean, jnp.float32))


def norm_step(z, gathered, after):
    return pl.pallas_call(
        functools.partial(norm_kernel, z),
        out_shape=jax.ShapeDtypeStruct((1, z.block), jnp.float32),
        in_specs=[VMEM, HBM],
        out_specs=VMEM,
        compiler_params=PARAMS,
        name="norm",
    )(gathered, after)


def swaps(pairs):
    return [pair for i, j in pairs for pair in ((i, j), (j, i))]


def per_device(margin, factor, pattern):
    slabs = lax.axis_size("slab")
    devices = lax.axis_size("grp") * slabs
    z = Sizes(margin.shape, margin.shape[0] * slabs, devices)
    if slabs % 2 or z.columns != 2 * z.half:
        raise ValueError("sizes")
    near_pairs = [(i, i + 1) for i in range(0, devices - 1, 2)]
    far_pairs = [(i, i + 1) for i in range(1, devices - 1, 2)]
    inner_pairs = [(i, j) for i, j in far_pairs if j % slabs]
    cross_pairs = [(i, j) for i, j in far_pairs if not j % slabs]
    mask_near = masks(z, pattern, margin.dtype)
    near, far, cross = pack(z, margin, factor, pattern, mask_near)
    beyond = lax.ppermute(far, AXES, swaps(inner_pairs))
    across = lax.ppermute(cross, AXES, swaps(cross_pairs))
    beside = lax.ppermute(near, AXES, swaps(near_pairs))
    z_cols, turned, p_part, d_part, squares, held16, held32 = inner_step(
        z, pattern, mask_near, near, far, beside
    )
    d_out, carry, spread = outer_step(
        z, pattern, beyond, across, z_cols, turned, p_part, d_part, squares
    )
    gathered = lax.all_to_all(spread, AXES, 0, 0, tiled=True)
    d_in = lax.ppermute(d_out, AXES, swaps(far_pairs))
    refined, held16, _, carry = middle_step(z, pattern, held16, held32, carry)
    refined, held16, _, _ = last_step(z, pattern, held16, carry, d_in, refined)
    norm = norm_step(z, gathered, held16)
    return refined, norm[0, 0]


def solution(mesh):
    return jax.shard_map(
        per_device,
        mesh=mesh,
        in_specs=(
            P(AXES, None, None, None),
            P(AXES, None, None, None),
            P(AXES, None),
        ),
        out_specs=(P(AXES, None, None, None), P()),
        check_vma=False,
    )
```

profile of v0, /device:TPU:0, one launch (start us, length us, event | category | flops | bytes accessed | tf_op | source)
XLA Modules:
  0.0 37.5 jit_solution(13349688293803441059)
XLA Ops:
  0.6 0.0 copy-start
  0.6 0.0 copy-start.2
  0.7 0.7 %copy-done.2 = s32[4,5]{1,0:T(4,128)S(1)} copy-done((s32[4,5]{1,0:T(4,128)S(1)}, s32[4,5]{1,0:T(4,128)}, u32[]{:S(2)}) %copy-start.2) | copy-done | bytes 104
  1.4 0.0 copy-start.1
  1.4 0.6 %masks.1._.mask_near = bf16[3,256,256]{2,1,0:T(8,128)(2,1)S(1)} custom-call(s32[4,5]{1,0:T(4,128)S(1)} %copy-done.2), custom_call_target="tpu_custom_call" | custom-call | flops 671088640 | bytes 1048576 | tf_op jit(solution)/shard_map/masks/pallas_call | solution.py:151
  2.0 0.0 copy-done
  2.0 0.5 %copy-done.1 = bf16[4,5,128,128]{3,2,1,0:T(8,128)(2,1)S(1)} copy-done((bf16[4,5,128,128]{3,2,1,0:T(8,128)(2,1)S(1)}, bf16[4,5,128,128]{3,2,1,0:T(8,128)(2,1)}, u32[]{:S(2)}) %copy-start.1) | copy-done | bytes 655384
  2.5 0.9 %pack.1 = (bf16[31,128,128]{2,1,0:T(8,128)(2,1)S(1)}, bf16[20,128,128]{2,1,0:T(8,128)(2,1)S(1)}, bf16[2,2,128,128]{3,2,1,0:T(8,128)(2,1)S(1)}) custom-call(bf16[4,5,128,128]{3,2,1,0:T(8,128)(2,1)S(1)} %copy-done, bf16[4,5,128,128]{3,2,1,0:T(8,128)(2,1)S(1)} %copy-done.1, s32[4,5]{1,0:T(4,128)S(1)} %copy-done.2, bf16[3,256,256]{2,1,0:T(8,128)(2,1)S(1)} %masks.1._.mask_near), custom_call_target="tpu_custom_call" | custom-call | tf_op jit(solution)/shard_map/pack/pallas_call | solution.py:198
  3.5 0.5 %collective-permute-start = (bf16[31,128,128]{2,1,0:T(8,128)(2,1)S(1)}, bf16[31,128,128]{2,1,0:T(8,128)(2,1)S(1)}, u32[]{:S(2)}, u32[]{:S(2)}) collective-permute-start(bf16[31,128,128]{2,1,0:T(8,128)(2,1)S(1)} %get-tuple-element.20.near), channel_id=1, source_target_pairs={{0,1},{1,0},{2,3},{3,2},{4,5},{5,4},{6,7},{7,6},{8,9},{9,8},{10,11... | collective-permute-start | bytes 3047432 | tf_op jit(solution)/shard_map/ppermute | solution.py:590
  4.0 0.7 %collective-permute-start.1 = (bf16[20,128,128]{2,1,0:T(8,128)(2,1)S(1)}, bf16[20,128,128]{2,1,0:T(8,128)(2,1)S(1)}, u32[]{:S(2)}, u32[]{:S(2)}) collective-permute-start(bf16[20,128,128]{2,1,0:T(8,128)(2,1)S(1)} %get-tuple-element.21.far), channel_id=1, source_target_pairs={{1,2},{2,1},{3,4},{4,3},{5,6},{6,5},{9,10},{10,9},{11,12},{12,11},... | collective-permute-start | bytes 1966088 | tf_op jit(solution)/shard_map/ppermute | solution.py:588
  4.7 0.7 %collective-permute-start.2 = (bf16[2,2,128,128]{3,2,1,0:T(8,128)(2,1)S(1)}, bf16[2,2,128,128]{3,2,1,0:T(8,128)(2,1)S(1)}, u32[]{:S(2)}, u32[]{:S(2)}) collective-permute-start(bf16[2,2,128,128]{3,2,1,0:T(8,128)(2,1)S(1)} %get-tuple-element.24), channel_id=1, source_target_pairs={{7,8},{8,7},{15,16},{16,15},{23,24},{24,23}} | collective-permute-start | bytes 393224 | tf_op jit(solution)/shard_map/ppermute | solution.py:589
  5.4 0.9 %collective-permute-done.beside = bf16[31,128,128]{2,1,0:T(8,128)(2,1)S(1)} collective-permute-done((bf16[31,128,128]{2,1,0:T(8,128)(2,1)S(1)}, bf16[31,128,128]{2,1,0:T(8,128)(2,1)S(1)}, u32[]{:S(2)}, u32[]{:S(2)}) %collective-permute-start) | collective-permute-done | bytes 1015840 | tf_op jit(solution)/shard_map/ppermute | solution.py:590
  6.2 3.9 %inner.1 = (bf16[3,3,256,256]{3,2,1,0:T(8,128)(2,1)S(1)}, bf16[3,256,256]{2,1,0:T(8,128)(2,1)S(1)}, f32[2,256,256]{2,1,0:T(8,128)S(1)}, f32[2,256,256]{2,1,0:T(8...) custom-call(s32[4,5]{1,0:T(4,128)S(1)} %copy-done.2, ...), custom_call_target="tpu_custom_call" | custom-call | flops 1811939328 | bytes 8388608 | tf_op jit(solution)/shard_map/inner/pallas_call | solution.py:315
  10.1 0.0 collective-permute-done.2.cross
  10.2 0.0 collective-permute-done.1.far
  10.2 2.8 %outer.1 = (bf16[2,256,256]{2,1,0:T(8,128)(2,1)}, bf16[5,256,256]{2,1,0:T(8,128)(2,1)S(1)}, f32[32,1,128]{2,1,0:T(1,128)S(1)}) custom-call(s32[4,5]{1,0:T(4,128)S(1)} %copy-done.2, bf16[20,128,128]{2,1,0:T(8,128)(2,1)S(1)} %collective-permute-done.1.far, bf16[2,2,128,128]{3,2,1,0:T(8,128)(2,1)S(1)} %collective-permute-done.2.cross, ...), custom_call_target="tpu_custom_call" | custom-call | flops 301989888 | bytes 4194304 | tf_op jit(solution)/shard_map/outer/pallas_call | solution.py:394
  12.9 0.0 copy-start.4
  12.9 0.6 %copy-done.4 = f32[32,1,128]{2,1,0:T(1,128)} copy-done((f32[32,1,128]{2,1,0:T(1,128)}, f32[32,1,128]{2,1,0:T(1,128)S(1)}, u32[]{:S(2)}) %copy-start.4) | copy-done | bytes 16408
  13.5 1.4 %collective-permute-start.3 = (bf16[2,256,256]{2,1,0:T(8,128)(2,1)}, bf16[2,256,256]{2,1,0:T(8,128)(2,1)}, u32[]{:S(2)}, u32[]{:S(2)}) collective-permute-start(bf16[2,256,256]{2,1,0:T(8,128)(2,1)} %get-tuple-element.33), channel_id=1, source_target_pairs={{1,2},{2,1},{3,4},{4,3},{5,6},{6,5},{7,8},{8,7},{9,10},{10,9},{11,... | collective-permute-start | bytes 786440 | tf_op jit(solution)/shard_map/ppermute | solution.py:598
  14.9 14.8 %all-to-all-start = ((f32[32,1,128]{2,1,0:T(1,128)}), f32[32,1,128]{2,1,0:T(1,128)S(1)}, u32[]{:S(2)}, u32[]{:S(2)}) async-start(f32[32,1,128]{2,1,0:T(1,128)} %copy-done.4), calls=%async_computation | async-start | bytes 32768 | tf_op jit(solution)/shard_map/all_to_all | solution.py:597
  29.7 0.0 copy-start.3
  29.7 0.7 %copy-done.3 = s32[4,5]{1,0:T(4,128)S(1)} copy-done((s32[4,5]{1,0:T(4,128)S(1)}, s32[4,5]{1,0:T(4,128)}, u32[]{:S(2)}) %copy-start.3) | copy-done | bytes 104
  30.4 2.2 %middle.1 = (bf16[4,5,128,128]{3,2,1,0:T(8,128)(2,1)}, bf16[10,256,256]{2,1,0:T(8,128)(2,1)S(1)}, f32[6,256,256]{2,1,0:T(8,128)S(1)}, bf16[5,256,256]{2,1,0:T(8,128)(2,1)S(1)}) custom-call(s32[4,5]{1,0:T(4,128)S(1)} %copy-done.3, bf16[10,256,256]{2,1,0:T(8,128)(2,1)S(1)} %get-tuple-element.22.held16_in, ...), custom_call_target="tpu_custom_call", output_to_operand_aliasing={{1}: (1, {}), {2}: (2, {}), {3}: (3, {})} | custom-call | flops 301989888 | bytes 6291456 | tf_op jit(solution)/shard_map/middle/pallas_call | solution.py:457
  32.6 0.0 collective-permute-done.3.d_in
  32.6 2.9 %last.1 = (bf16[4,5,128,128]{3,2,1,0:T(8,128)(2,1)}, bf16[10,256,256]{2,1,0:T(8,128)(2,1)S(1)}, bf16[5,256,256]{2,1,0:T(8,128)(2,1)S(1)}, bf16[2,256,256]{2,1,0:T(8,128)(2,1)}) custom-call(s32[4,5]{1,0:T(4,128)S(1)} %copy-done.3, ...), custom_call_target="tpu_custom_call", output_to_operand_aliasing={{0}: (4, {}), {1}: (1, {}), {2}: (2, {}), {3}: (3, {})} | custom-call | flops 704643072 | bytes 4194304 | tf_op jit(solution)/shard_map/last/pallas_call | solution.py:533
  35.5 1.4 %all-to-all-done.gathered = f32[32,1,128]{2,1,0:T(1,128)S(1)} async-done(((f32[32,1,128]{2,1,0:T(1,128)}), f32[32,1,128]{2,1,0:T(1,128)S(1)}, u32[]{:S(2)}, u32[]{:S(2)}) %all-to-all-start) | async-done | bytes 16416 | tf_op jit(solution)/shard_map/all_to_all | solution.py:597
  36.8 0.7 %norm.1 = f32[1,128]{1,0:T(1,128)} custom-call(f32[32,1,128]{2,1,0:T(1,128)S(1)} %all-to-all-done.gathered, bf16[10,256,256]{2,1,0:T(8,128)(2,1)S(1)} %get-tuple-element.37._), custom_call_target="tpu_custom_call" | custom-call | tf_op jit(solution)/shard_map/norm/pallas_call | solution.py:562
Async XLA Ops:
  0.6 1.4 %copy-start = (bf16[4,5,128,128]{3,2,1,0:T(8,128)(2,1)S(1)}, bf16[4,5,128,128]{3,2,1,0:T(8,128)(2,1)}, u32[]{:S(2)}) copy-start(bf16[4,5,128,128]{3,2,1,0:T(8,128)(2,1)} %margin.1) | copy-start | bytes 1966084
  0.6 0.7 %copy-start.2 = (s32[4,5]{1,0:T(4,128)S(1)}, s32[4,5]{1,0:T(4,128)}, u32[]{:S(2)}) copy-start(s32[4,5]{1,0:T(4,128)} %pattern_in.3) | copy-start | bytes 244
  1.4 1.1 %copy-start.1 = (bf16[4,5,128,128]{3,2,1,0:T(8,128)(2,1)S(1)}, bf16[4,5,128,128]{3,2,1,0:T(8,128)(2,1)}, u32[]{:S(2)}) copy-start(bf16[4,5,128,128]{3,2,1,0:T(8,128)(2,1)} %factor.1) | copy-start | bytes 1966084
  3.5 2.8 %collective-permute-start = (bf16[31,128,128]{2,1,0:T(8,128)(2,1)S(1)}, bf16[31,128,128]{2,1,0:T(8,128)(2,1)S(1)}, u32[]{:S(2)}, u32[]{:S(2)}) collective-permute-start(bf16[31,128,128]{2,1,0:T(8,128)(2,1)S(1)} %get-tuple-element.20.near), channel_id=1, source_target_pairs={{0,1},{1,0},{2,3},{3,2},{4,5},{5,4},{6,7},{7,6},{8,9},{9,8},{10,11... | collective-permute-start | bytes 3047432 | tf_op jit(solution)/shard_map/ppermute | solution.py:590
  4.0 6.2 %collective-permute-start.1 = (bf16[20,128,128]{2,1,0:T(8,128)(2,1)S(1)}, bf16[20,128,128]{2,1,0:T(8,128)(2,1)S(1)}, u32[]{:S(2)}, u32[]{:S(2)}) collective-permute-start(bf16[20,128,128]{2,1,0:T(8,128)(2,1)S(1)} %get-tuple-element.21.far), channel_id=1, source_target_pairs={{1,2},{2,1},{3,4},{4,3},{5,6},{6,5},{9,10},{10,9},{11,12},{12,11},... | collective-permute-start | bytes 1966088 | tf_op jit(solution)/shard_map/ppermute | solution.py:588
  4.7 5.5 %collective-permute-start.2 = (bf16[2,2,128,128]{3,2,1,0:T(8,128)(2,1)S(1)}, bf16[2,2,128,128]{3,2,1,0:T(8,128)(2,1)S(1)}, u32[]{:S(2)}, u32[]{:S(2)}) collective-permute-start(bf16[2,2,128,128]{3,2,1,0:T(8,128)(2,1)S(1)} %get-tuple-element.24), channel_id=1, source_target_pairs={{7,8},{8,7},{15,16},{16,15},{23,24},{24,23}} | collective-permute-start | bytes 393224 | tf_op jit(solution)/shard_map/ppermute | solution.py:589
  12.9 0.6 %copy-start.4 = (f32[32,1,128]{2,1,0:T(1,128)}, f32[32,1,128]{2,1,0:T(1,128)S(1)}, u32[]{:S(2)}) copy-start(f32[32,1,128]{2,1,0:T(1,128)S(1)} %get-tuple-element.36) | copy-start | bytes 49156
  13.5 19.0 %collective-permute-start.3 = (bf16[2,256,256]{2,1,0:T(8,128)(2,1)}, bf16[2,256,256]{2,1,0:T(8,128)(2,1)}, u32[]{:S(2)}, u32[]{:S(2)}) collective-permute-start(bf16[2,256,256]{2,1,0:T(8,128)(2,1)} %get-tuple-element.33), channel_id=1, source_target_pairs={{1,2},{2,1},{3,4},{4,3},{5,6},{6,5},{7,8},{8,7},{9,10},{10,9},{11,... | collective-permute-start | bytes 786440 | tf_op jit(solution)/shard_map/ppermute | solution.py:598
  14.9 22.0 %all-to-all-start = ((f32[32,1,128]{2,1,0:T(1,128)}), f32[32,1,128]{2,1,0:T(1,128)S(1)}, u32[]{:S(2)}, u32[]{:S(2)}) async-start(f32[32,1,128]{2,1,0:T(1,128)} %copy-done.4), calls=%async_computation | async-start | bytes 32768 | tf_op jit(solution)/shard_map/all_to_all | solution.py:597
  29.7 0.7 %copy-start.3 = (s32[4,5]{1,0:T(4,128)S(1)}, s32[4,5]{1,0:T(4,128)}, u32[]{:S(2)}) copy-start(s32[4,5]{1,0:T(4,128)} %pattern_in.3) | copy-start | bytes 244
where the time goes:
time: 37.8 us; the launch traced here: 37.5 us
  starting transfers between devices  18 us (48%)
  Pallas kernels  13.9 us (37%)
  local copies, waits for them, and re-layouts  2.51 us (7%)
  waiting for transfers between devices  2.25 us (6%)
  between operations  0.77 us (2%)
    all_to_all x1, starting transfers between devices, per_device(): gathered = lax.all_to_all(spread, AXES, 0, 0, tiled=True)  14.8 us
    pallas_call x1, Pallas kernels, inner_step(): pl.pallas_call(functools.partial(inner_kernel, z), out_shape=(jax.ShapeDt...  3.92 us
    pallas_call x1, Pallas kernels, last_step(): pl.pallas_call(functools.partial(last_kernel, z), out_shape=tuple((jax.Sh...  2.89 us
    pallas_call x1, Pallas kernels, outer_step(): pl.pallas_call(functools.partial(outer_kernel, z), out_shape=(z.tiles(2,...  2.76 us
    unnamed x10, local copies, waits for them, and re-layouts  2.51 us
    pallas_call x1, Pallas kernels, middle_step(): pl.pallas_call(functools.partial(middle_kernel, z), out_shape=(jax.ShapeD...  2.16 us
    all_to_all x1, waiting for transfers between devices, per_device(): gathered = lax.all_to_all(spread, AXES, 0, 0, tiled=True)  1.38 us
    ppermute x1, starting transfers between devices, per_device(): d_in = lax.ppermute(d_out, AXES, swaps(far_pairs))  1.36 us
  transfers between devices with their start and end apart: 5, of which 2 were waited for; matrix products, arithmetic and copies ran while one was open for 0% of the time, Pallas kernels for 24%

commit v1 on v0

--- a/solution.py
+++ b/solution.py
@@ -211,7 +211,7 @@
 
 def inner_kernel(
     z, pattern, mask_near, near, far, beside, z_cols, turned, p_part, d_part, squares, held16, held32,
-    s_cols, z_turned, image, d_near, d_beside, sums, sems,
+    flags, s_cols, z_turned, image, d_near, d_beside, sums, sems,
 ):
     near_first, _ = half_starts(z)
     kind = near.dtype
@@ -230,13 +230,14 @@
         (z_cols.at[0], held16.at[pl.ds(2, 3)]),
         (z_cols.at[1], held16.at[pl.ds(5, 3)]),
         (z_cols.at[2, pl.ds(0, 2)], held16.at[pl.ds(8, 2)]),
+        (pattern, flags),
         (d_near.at[pl.ds(0, 2)], held16.at[pl.ds(0, 2)]),
         (sums, held32),
     ]
     copies = [
         pltpu.make_async_copy(source, target, sems.at[k]) for k, (source, target) in enumerate(moves)
     ]
-    for copy in copies[:3]:
+    for copy in copies[:4]:
         copy.start()
     for x in range(3):
         for e in range(3):
@@ -276,7 +277,7 @@
         d_near[i - 1] = value
         total = total + sum_squares(z, value)
     squares[...] = total
-    copies[3].start()
+    copies[4].start()
 
     def side_flag(t, u):
         o = offset_of(z, 0, t, u)
@@ -304,7 +305,7 @@
             factor, d_near, i, 2, 1, 3
         )
         sums[2 + i] = tile_product(defect, d_near, i, 2, 2, 3)
-    copies[4].start()
+    copies[5].start()
     for copy in copies:
         copy.wait()
 
@@ -322,9 +323,10 @@
             jax.ShapeDtypeStruct((8, tile), jnp.float32),
             z.tiles(10, kind),
             z.tiles(6, jnp.float32),
+            jax.ShapeDtypeStruct(pattern.shape, pattern.dtype),
         ),
         in_specs=[SMEM, VMEM, VMEM, VMEM, VMEM],
-        out_specs=(VMEM,) * 5 + (HBM,) * 2,
+        out_specs=(VMEM,) * 5 + (HBM,) * 3,
         scratch_shapes=[
             pltpu.VMEM((4, 3, tile, tile), kind),
             pltpu.VMEM((3, 3, tile, tile), kind),
@@ -332,7 +334,7 @@
             pltpu.VMEM((3, tile, tile), kind),
             pltpu.VMEM((2, tile, tile), kind),
             pltpu.VMEM((6, tile, tile), jnp.float32),
-            pltpu.SemaphoreType.DMA((5,)),
+            pltpu.SemaphoreType.DMA((6,)),
         ],
         compiler_params=PARAMS,
         cost_estimate=z.cost(54, 8),
@@ -341,8 +343,8 @@
 
 
 def outer_kernel(
-    z, pattern, far, cross, z_cols, turned, p_part, d_part, squares, d_out, carry, spread, s_far, z_far,
-    d_far, sems,
+    z, pattern, far, cross, z_cols, turned, p_part, d_part, squares, d_out, carry, spread_out, s_far,
+    z_far, d_far, spread, sems,
 ):
     _, far_first = half_starts(z)
     kind = far.dtype
@@ -356,8 +358,13 @@
 
     expand(z, s_far, lambda t, o: far[t * z.offsets + o])
     expand(z, z_far, factor_cell)
-    copies = [pltpu.make_async_copy(z_far.at[pl.ds(1, 2)], carry.at[pl.ds(0, 2)], sems.at[0])]
-    copies[0].start()
+    copies = []
+
+    def send(source, target):
+        copies.append(pltpu.make_async_copy(source, target, sems.at[len(copies)]))
+        copies[-1].start()
+
+    send(z_far.at[pl.ds(1, 2)], carry.at[pl.ds(0, 2)])
     link = z_cols[0, 0]
     image = (
         dot(s_far[0], link).astype(kind),
@@ -373,18 +380,16 @@
     for e, value in enumerate(values):
         value = own_masked(z, pattern, far_first, e, value).astype(kind)
         d_far[e] = value
-        copies.append(
-            pltpu.make_async_copy(d_far.at[pl.ds(e, 1)], carry.at[pl.ds(2 + e, 1)], sems.at[1 + e])
-        )
-        copies[-1].start()
-        if e < 2:
-            d_out[e] = value
         total = total + sum_squares(z, value)
+        if e == 1:
+            send(d_far.at[pl.ds(0, 2)], d_out)
+    send(d_far, carry.at[pl.ds(2, 3)])
     lanes = jnp.sum(total, axis=0, keepdims=True)
     folded = lanes[:, : z.block]
     for t in range(1, z.half):
         folded = folded + lanes[:, t * z.block : (t + 1) * z.block]
     spread[...] = jnp.broadcast_to(folded[None], spread.shape)
+    send(spread, spread_out)
     for copy in copies:
         copy.wait()
 
@@ -399,11 +404,12 @@
             jax.ShapeDtypeStruct((z.devices, 1, z.block), jnp.float32),
         ),
         in_specs=[SMEM] + [VMEM] * 7,
-        out_specs=(VMEM, HBM, VMEM),
+        out_specs=(HBM, HBM, HBM),
         scratch_shapes=[
             pltpu.VMEM((3, z.tile, z.tile), kind),
             pltpu.VMEM((3, z.tile, z.tile), kind),
             pltpu.VMEM((3, z.tile, z.tile), kind),
+            pltpu.VMEM((z.devices, 1, z.block), jnp.float32),
             pltpu.SemaphoreType.DMA((4,)),
         ],
         compiler_params=PARAMS,
@@ -413,7 +419,7 @@
 
 
 def middle_kernel(
-    z, pattern_in, held16_in, held32_in, carry_in, refined, _a, _b, _c, pattern, held16, held32, d_far,
+    z, pattern_in, held16_in, held32_in, carry_in, refined, _a, _b, _c, _d, pattern, held16, held32, d_far,
     square, tiles, cells, sems,
 ):
     first, _ = half_starts(z)
@@ -461,9 +467,10 @@
             jax.ShapeDtypeStruct(held16.shape, kind),
             jax.ShapeDtypeStruct(held32.shape, jnp.float32),
             jax.ShapeDtypeStruct(carry.shape, kind),
+            jax.ShapeDtypeStruct(pattern.shape, pattern.dtype),
         ),
         in_specs=[HBM] * 4,
-        out_specs=(HBM,) * 4,
+        out_specs=(HBM,) * 5,
         scratch_shapes=[
             pltpu.SMEM(pattern.shape, pattern.dtype),
             pltpu.VMEM(held16.shape, kind),
@@ -474,7 +481,7 @@
             pltpu.VMEM((z.half,) + shape[1:], kind),
             pltpu.SemaphoreType.DMA((7,)),
         ],
-        input_output_aliases={1: 1, 2: 2, 3: 3},
+        input_output_aliases={1: 1, 2: 2, 3: 3, 0: 4},
         compiler_params=PARAMS,
         cost_estimate=z.cost(9, 6),
         name="middle",
@@ -482,8 +489,8 @@
 
 
 def last_kernel(
-    z, pattern_in, held16, carry, d_in, _, refined, _a, _b, _c, pattern, narrow, d_beyond, square, tiles,
-    cells, sems,
+    z, pattern_in, held16, carry, d_in, _, refined, _a, _b, _c, _d, pattern, narrow, d_beyond, square,
+    tiles, cells, sems,
 ):
     _, first = half_starts(z)
     moves = (
@@ -533,10 +540,10 @@
     return pl.pallas_call(
         functools.partial(last_kernel, z),
         out_shape=tuple(
-            jax.ShapeDtypeStruct(held.shape, held.dtype) for held in (refined, held16, carry, d_in)
+            jax.ShapeDtypeStruct(held.shape, held.dtype) for held in (refined, held16, carry, d_in, pattern)
         ),
         in_specs=[HBM] * 5,
-        out_specs=(HBM,) * 4,
+        out_specs=(HBM,) * 5,
         scratch_shapes=[
             pltpu.SMEM(pattern.shape, pattern.dtype),
             pltpu.VMEM((12, z.tile, z.tile), kind),
@@ -546,7 +553,7 @@
             pltpu.VMEM((z.half,) + refined.shape[1:], kind),
             pltpu.SemaphoreType.DMA((7,)),
         ],
-        input_output_aliases={4: 0, 1: 1, 2: 2, 3: 3},
+        input_output_aliases={4: 0, 1: 1, 2: 2, 3: 3, 0: 4},
         compiler_params=PARAMS,
         cost_estimate=z.cost(21, 4),
         name="last",
@@ -588,7 +595,7 @@
     beyond = lax.ppermute(far, AXES, swaps(inner_pairs))
     across = lax.ppermute(cross, AXES, swaps(cross_pairs))
     beside = lax.ppermute(near, AXES, swaps(near_pairs))
-    z_cols, turned, p_part, d_part, squares, held16, held32 = inner_step(
+    z_cols, turned, p_part, d_part, squares, held16, held32, flags = inner_step(
         z, pattern, mask_near, near, far, beside
     )
     d_out, carry, spread = outer_step(
@@ -596,8 +603,8 @@
     )
     gathered = lax.all_to_all(spread, AXES, 0, 0, tiled=True)
     d_in = lax.ppermute(d_out, AXES, swaps(far_pairs))
-    refined, held16, _, carry = middle_step(z, pattern, held16, held32, carry)
-    refined, held16, _, _ = last_step(z, pattern, held16, carry, d_in, refined)
+    refined, held16, _, carry, flags = middle_step(z, flags, held16, held32, carry)
+    refined, held16, _, _, _ = last_step(z, flags, held16, carry, d_in, refined)
     norm = norm_step(z, gathered, held16)
     return refined, norm[0, 0]
 

time: 37.8 us -> 37.2 us (0.984)
  Pallas kernels: 13.9 us -> 13.3 us
    pallas_call x1, Pallas kernels: 2.76 us -> 2.12 us  [outer_step(): pl.pallas_call(functools.partial(outer_kernel, z), out_shape=(z.tiles(2,...]
    unnamed x10 -> x14, local copies, waits for them, and re-layouts: 2.51 us -> 2.51 us
where the time goes in v1:
time: 37.2 us; the launch traced here: 36.9 us
  starting transfers between devices  18.1 us (49%)
  Pallas kernels  13.3 us (36%)
  local copies, waits for them, and re-layouts  2.51 us (7%)
  waiting for transfers between devices  2.26 us (6%)
  between operations  0.79 us (2%)
    all_to_all x1, starting transfers between devices, per_device(): gathered = lax.all_to_all(spread, AXES, 0, 0, tiled=True)  14.8 us
    pallas_call x1, Pallas kernels, inner_step(): pl.pallas_call(functools.partial(inner_kernel, z), out_shape=(jax.ShapeDt...  3.89 us
    pallas_call x1, Pallas kernels, last_step(): pl.pallas_call(functools.partial(last_kernel, z), out_shape=tuple((jax.Sh...  2.89 us
    unnamed x14, local copies, waits for them, and re-layouts  2.51 us
    pallas_call x1, Pallas kernels, middle_step(): pl.pallas_call(functools.partial(middle_kernel, z), out_shape=(jax.ShapeD...  2.16 us
    pallas_call x1, Pallas kernels, outer_step(): pl.pallas_call(functools.partial(outer_kernel, z), out_shape=(z.tiles(2,...  2.12 us
    all_to_all x1, waiting for transfers between devices, per_device(): gathered = lax.all_to_all(spread, AXES, 0, 0, tiled=True)  1.39 us
    ppermute x1, starting transfers between devices, per_device(): d_in = lax.ppermute(d_out, AXES, swaps(far_pairs))  1.35 us
  transfers between devices with their start and end apart: 5, of which 2 were waited for; matrix products, arithmetic and copies ran while one was open for 0% of the time, Pallas kernels for 24%

profile of v1, /device:TPU:0, one launch (start us, length us, event | category | flops | bytes accessed | tf_op | source)
XLA Modules:
  0.0 36.9 jit_solution(6872392241384907472)
XLA Ops:
  0.6 0.0 copy-start
  0.6 0.0 copy-start.3
  0.6 0.7 %copy-done.3 = s32[4,5]{1,0:T(4,128)S(1)} copy-done((s32[4,5]{1,0:T(4,128)S(1)}, s32[4,5]{1,0:T(4,128)}, u32[]{:S(2)}) %copy-start.3) | copy-done | bytes 104
  1.4 0.0 copy-start.1
  1.4 0.0 copy-start.4
  1.4 0.6 %masks.1._.mask_near = bf16[3,256,256]{2,1,0:T(8,128)(2,1)S(1)} custom-call(s32[4,5]{1,0:T(4,128)S(1)} %copy-done.3), custom_call_target="tpu_custom_call" | custom-call | flops 671088640 | bytes 1048576 | tf_op jit(solution)/shard_map/masks/pallas_call | solution.py:151
  2.0 0.0 copy-done
  2.0 0.5 %copy-done.1 = bf16[4,5,128,128]{3,2,1,0:T(8,128)(2,1)S(1)} copy-done((bf16[4,5,128,128]{3,2,1,0:T(8,128)(2,1)S(1)}, bf16[4,5,128,128]{3,2,1,0:T(8,128)(2,1)}, u32[]{:S(2)}) %copy-start.1) | copy-done | bytes 655384
  2.5 0.0 copy-done.4
  2.5 0.9 %pack.1 = (bf16[31,128,128]{2,1,0:T(8,128)(2,1)S(1)}, bf16[20,128,128]{2,1,0:T(8,128)(2,1)S(1)}, bf16[2,2,128,128]{3,2,1,0:T(8,128)(2,1)S(1)}) custom-call(bf16[4,5,128,128]{3,2,1,0:T(8,128)(2,1)S(1)} %copy-done, bf16[4,5,128,128]{3,2,1,0:T(8,128)(2,1)S(1)} %copy-done.1, s32[4,5]{1,0:T(4,128)S(1)} %copy-done.4, bf16[3,256,256]{2,1,0:T(8,128)(2,1)S(1)} %masks.1._.mask_near), custom_call_target="tpu_custom_call" | custom-call | tf_op jit(solution)/shard_map/pack/pallas_call | solution.py:198
  3.5 0.5 %collective-permute-start = (bf16[31,128,128]{2,1,0:T(8,128)(2,1)S(1)}, bf16[31,128,128]{2,1,0:T(8,128)(2,1)S(1)}, u32[]{:S(2)}, u32[]{:S(2)}) collective-permute-start(bf16[31,128,128]{2,1,0:T(8,128)(2,1)S(1)} %get-tuple-element.22.near), channel_id=1, source_target_pairs={{0,1},{1,0},{2,3},{3,2},{4,5},{5,4},{6,7},{7,6},{8,9},{9,8},{10,11... | collective-permute-start | bytes 3047432 | tf_op jit(solution)/shard_map/ppermute | solution.py:597
  4.0 0.7 %collective-permute-start.1 = (bf16[20,128,128]{2,1,0:T(8,128)(2,1)S(1)}, bf16[20,128,128]{2,1,0:T(8,128)(2,1)S(1)}, u32[]{:S(2)}, u32[]{:S(2)}) collective-permute-start(bf16[20,128,128]{2,1,0:T(8,128)(2,1)S(1)} %get-tuple-element.23.far), channel_id=1, source_target_pairs={{1,2},{2,1},{3,4},{4,3},{5,6},{6,5},{9,10},{10,9},{11,12},{12,11},... | collective-permute-start | bytes 1966088 | tf_op jit(solution)/shard_map/ppermute | solution.py:595
  4.7 0.7 %collective-permute-start.2 = (bf16[2,2,128,128]{3,2,1,0:T(8,128)(2,1)S(1)}, bf16[2,2,128,128]{3,2,1,0:T(8,128)(2,1)S(1)}, u32[]{:S(2)}, u32[]{:S(2)}) collective-permute-start(bf16[2,2,128,128]{3,2,1,0:T(8,128)(2,1)S(1)} %get-tuple-element.27), channel_id=1, source_target_pairs={{7,8},{8,7},{15,16},{16,15},{23,24},{24,23}} | collective-permute-start | bytes 393224 | tf_op jit(solution)/shard_map/ppermute | solution.py:596
  5.4 0.9 %collective-permute-done.beside = bf16[31,128,128]{2,1,0:T(8,128)(2,1)S(1)} collective-permute-done((bf16[31,128,128]{2,1,0:T(8,128)(2,1)S(1)}, bf16[31,128,128]{2,1,0:T(8,128)(2,1)S(1)}, u32[]{:S(2)}, u32[]{:S(2)}) %collective-permute-start) | collective-permute-done | bytes 1015840 | tf_op jit(solution)/shard_map/ppermute | solution.py:597
  6.2 3.9 %inner.1 = (bf16[3,3,256,256]{3,2,1,0:T(8,128)(2,1)S(1)}, bf16[3,256,256]{2,1,0:T(8,128)(2,1)S(1)}, f32[2,256,256]{2,1,0:T(8,128)S(1)}, f32[2,256,256]{2,1,0:T(8...) custom-call(s32[4,5]{1,0:T(4,128)S(1)} %copy-done.4, ...), custom_call_target="tpu_custom_call" | custom-call | flops 1811939328 | bytes 8388608 | tf_op jit(solution)/shard_map/inner/pallas_call | solution.py:316
  10.1 0.0 copy-start.5
  10.1 0.0 collective-permute-done.2.cross
  10.1 0.0 collective-permute-done.1.far
  10.2 2.1 %outer.1 = (bf16[2,256,256]{2,1,0:T(8,128)(2,1)}, bf16[5,256,256]{2,1,0:T(8,128)(2,1)S(1)}, f32[32,1,128]{2,1,0:T(1,128)S(1)}) custom-call(s32[4,5]{1,0:T(4,128)S(1)} %copy-done.4, bf16[20,128,128]{2,1,0:T(8,128)(2,1)S(1)} %collective-permute-done.1.far, bf16[2,2,128,128]{3,2,1,0:T(8,128)(2,1)S(1)} %collective-permute-done.2.cross, ...), custom_call_target="tpu_custom_call" | custom-call | flops 301989888 | bytes 4194304 | tf_op jit(solution)/shard_map/outer/pallas_call | solution.py:399
  12.3 0.0 copy-done.5
  12.3 0.0 copy-start.2
  12.3 0.6 %copy-done.2 = f32[32,1,128]{2,1,0:T(1,128)} copy-done((f32[32,1,128]{2,1,0:T(1,128)}, f32[32,1,128]{2,1,0:T(1,128)S(1)}, u32[]{:S(2)}) %copy-start.2) | copy-done | bytes 16408
  12.9 1.3 %collective-permute-start.3 = (bf16[2,256,256]{2,1,0:T(8,128)(2,1)}, bf16[2,256,256]{2,1,0:T(8,128)(2,1)}, u32[]{:S(2)}, u32[]{:S(2)}) collective-permute-start(bf16[2,256,256]{2,1,0:T(8,128)(2,1)} %get-tuple-element.37), channel_id=1, source_target_pairs={{1,2},{2,1},{3,4},{4,3},{5,6},{6,5},{7,8},{8,7},{9,10},{10,9},{11,... | collective-permute-start | bytes 786440 | tf_op jit(solution)/shard_map/ppermute | solution.py:605
  14.2 14.8 %all-to-all-start = ((f32[32,1,128]{2,1,0:T(1,128)}), f32[32,1,128]{2,1,0:T(1,128)S(1)}, u32[]{:S(2)}, u32[]{:S(2)}) async-start(f32[32,1,128]{2,1,0:T(1,128)} %copy-done.2), calls=%async_computation | async-start | bytes 32768 | tf_op jit(solution)/shard_map/all_to_all | solution.py:604
  29.1 0.0 copy-start.6
  29.1 0.7 %copy-done.6 = s32[4,5]{1,0:T(4,128)S(1)} copy-done((s32[4,5]{1,0:T(4,128)S(1)}, s32[4,5]{1,0:T(4,128)}, u32[]{:S(2)}) %copy-start.6) | copy-done | bytes 104
  29.8 2.2 %middle.1 = (bf16[4,5,128,128]{3,2,1,0:T(8,128)(2,1)}, bf16[10,256,256]{2,1,0:T(8,128)(2,1)S(1)}, f32[6,256,256]{2,1,0:T(8,128)S(1)}, bf16[5,256,256]{2,1,0:T(8,128)(2,1)S(1)}, s32[4,5]{1,0:T(4,128)S(1)}) custom-call(s32[4,5]{1,0:T(4,128)S(1)} %copy-done.6, ...), custom_call_target="tpu_custom_call", output_to_operand_aliasing={{1}: (1, {}), {2}: (2, {}), {3}: (3, {}), {4}: (0, {})} | custom-call | flops 301989888 | bytes 6291456 | tf_op jit(solution)/shard_map/middle/pallas_call | solution.py:463
  31.9 0.0 collective-permute-done.3.d_in
  31.9 2.9 %last.1 = (bf16[4,5,128,128]{3,2,1,0:T(8,128)(2,1)}, bf16[10,256,256]{2,1,0:T(8,128)(2,1)S(1)}, bf16[5,256,256]{2,1,0:T(8,128)(2,1)S(1)}, bf16[2,256,256]{2,1,0:T(8,128)(2,1)}, s32[4,5]{1,0:T(4,128)S(1)}) custom-call(s32[4,5]{1,0:T(4,128)S(1)} %get-tuple-element.34.pattern_in, ...), custom_call_target="tpu_custom_call", output_to_operand_aliasing={{0}: (4, {}), {1}: (1, {}), {2}: (2, {}), {3}: (3, {}), {4}... | custom-call | flops 704643072 | bytes 4194304 | tf_op jit(solution)/shard_map/last/pallas_call | solution.py:540
  34.8 1.4 %all-to-all-done.gathered = f32[32,1,128]{2,1,0:T(1,128)S(1)} async-done(((f32[32,1,128]{2,1,0:T(1,128)}), f32[32,1,128]{2,1,0:T(1,128)S(1)}, u32[]{:S(2)}, u32[]{:S(2)}) %all-to-all-start) | async-done | bytes 16416 | tf_op jit(solution)/shard_map/all_to_all | solution.py:604
  36.2 0.7 %norm.1 = f32[1,128]{1,0:T(1,128)} custom-call(f32[32,1,128]{2,1,0:T(1,128)S(1)} %all-to-all-done.gathered, bf16[10,256,256]{2,1,0:T(8,128)(2,1)S(1)} %get-tuple-element.41._), custom_call_target="tpu_custom_call" | custom-call | tf_op jit(solution)/shard_map/norm/pallas_call | solution.py:569
Async XLA Ops:
  0.6 1.4 %copy-start = (bf16[4,5,128,128]{3,2,1,0:T(8,128)(2,1)S(1)}, bf16[4,5,128,128]{3,2,1,0:T(8,128)(2,1)}, u32[]{:S(2)}) copy-start(bf16[4,5,128,128]{3,2,1,0:T(8,128)(2,1)} %margin.1) | copy-start | bytes 1966084
  0.6 0.7 %copy-start.3 = (s32[4,5]{1,0:T(4,128)S(1)}, s32[4,5]{1,0:T(4,128)}, u32[]{:S(2)}) copy-start(s32[4,5]{1,0:T(4,128)} %pattern.7) | copy-start | bytes 244
  1.4 1.1 %copy-start.1 = (bf16[4,5,128,128]{3,2,1,0:T(8,128)(2,1)S(1)}, bf16[4,5,128,128]{3,2,1,0:T(8,128)(2,1)}, u32[]{:S(2)}) copy-start(bf16[4,5,128,128]{3,2,1,0:T(8,128)(2,1)} %factor.1) | copy-start | bytes 1966084
  1.4 1.1 %copy-start.4 = (s32[4,5]{1,0:T(4,128)S(1)}, s32[4,5]{1,0:T(4,128)}, u32[]{:S(2)}) copy-start(s32[4,5]{1,0:T(4,128)} %pattern.7) | copy-start | bytes 244
  3.5 2.8 %collective-permute-start = (bf16[31,128,128]{2,1,0:T(8,128)(2,1)S(1)}, bf16[31,128,128]{2,1,0:T(8,128)(2,1)S(1)}, u32[]{:S(2)}, u32[]{:S(2)}) collective-permute-start(bf16[31,128,128]{2,1,0:T(8,128)(2,1)S(1)} %get-tuple-element.22.near), channel_id=1, source_target_pairs={{0,1},{1,0},{2,3},{3,2},{4,5},{5,4},{6,7},{7,6},{8,9},{9,8},{10,11... | collective-permute-start | bytes 3047432 | tf_op jit(solution)/shard_map/ppermute | solution.py:597
  4.0 6.2 %collective-permute-start.1 = (bf16[20,128,128]{2,1,0:T(8,128)(2,1)S(1)}, bf16[20,128,128]{2,1,0:T(8,128)(2,1)S(1)}, u32[]{:S(2)}, u32[]{:S(2)}) collective-permute-start(bf16[20,128,128]{2,1,0:T(8,128)(2,1)S(1)} %get-tuple-element.23.far), channel_id=1, source_target_pairs={{1,2},{2,1},{3,4},{4,3},{5,6},{6,5},{9,10},{10,9},{11,12},{12,11},... | collective-permute-start | bytes 1966088 | tf_op jit(solution)/shard_map/ppermute | solution.py:595
  4.7 5.5 %collective-permute-start.2 = (bf16[2,2,128,128]{3,2,1,0:T(8,128)(2,1)S(1)}, bf16[2,2,128,128]{3,2,1,0:T(8,128)(2,1)S(1)}, u32[]{:S(2)}, u32[]{:S(2)}) collective-permute-start(bf16[2,2,128,128]{3,2,1,0:T(8,128)(2,1)S(1)} %get-tuple-element.27), channel_id=1, source_target_pairs={{7,8},{8,7},{15,16},{16,15},{23,24},{24,23}} | collective-permute-start | bytes 393224 | tf_op jit(solution)/shard_map/ppermute | solution.py:596
  10.1 2.2 %copy-start.5 = (s32[4,5]{1,0:T(4,128)}, s32[4,5]{1,0:T(4,128)S(1)}, u32[]{:S(2)}) copy-start(s32[4,5]{1,0:T(4,128)S(1)} %get-tuple-element.24.pattern_in) | copy-start | bytes 244
  12.3 0.6 %copy-start.2 = (f32[32,1,128]{2,1,0:T(1,128)}, f32[32,1,128]{2,1,0:T(1,128)S(1)}, u32[]{:S(2)}) copy-start(f32[32,1,128]{2,1,0:T(1,128)S(1)} %get-tuple-element.40) | copy-start | bytes 49156
  12.9 19.0 %collective-permute-start.3 = (bf16[2,256,256]{2,1,0:T(8,128)(2,1)}, bf16[2,256,256]{2,1,0:T(8,128)(2,1)}, u32[]{:S(2)}, u32[]{:S(2)}) collective-permute-start(bf16[2,256,256]{2,1,0:T(8,128)(2,1)} %get-tuple-element.37), channel_id=1, source_target_pairs={{1,2},{2,1},{3,4},{4,3},{5,6},{6,5},{7,8},{8,7},{9,10},{10,9},{11,... | collective-permute-start | bytes 786440 | tf_op jit(solution)/shard_map/ppermute | solution.py:605
  14.2 22.0 %all-to-all-start = ((f32[32,1,128]{2,1,0:T(1,128)}), f32[32,1,128]{2,1,0:T(1,128)S(1)}, u32[]{:S(2)}, u32[]{:S(2)}) async-start(f32[32,1,128]{2,1,0:T(1,128)} %copy-done.2), calls=%async_computation | async-start | bytes 32768 | tf_op jit(solution)/shard_map/all_to_all | solution.py:604
  29.1 0.7 %copy-start.6 = (s32[4,5]{1,0:T(4,128)S(1)}, s32[4,5]{1,0:T(4,128)}, u32[]{:S(2)}) copy-start(s32[4,5]{1,0:T(4,128)} %copy-done.5) | copy-start | bytes 244

commit v2 on v1

--- a/solution.py
+++ b/solution.py
@@ -140,23 +140,19 @@
             cells[t, o] = value.astype(cells.dtype)
 
 
-def mask_kernel(z, pattern, mask_near):
-    first, _ = half_starts(z)
-    ones = jnp.ones((z.tile, z.tile), jnp.float32)
-    for e in range(3):
-        mask_near[e] = own_masked(z, pattern, first, e, ones).astype(mask_near.dtype)
-
-
-def masks(z, pattern, kind):
+def unit_kernel(z, unit):
+    unit[...] = identity(z)
+
+
+def unit_tile(z):
     return pl.pallas_call(
-        functools.partial(mask_kernel, z),
-        out_shape=z.tiles(3, kind),
-        in_specs=[SMEM],
+        functools.partial(unit_kernel, z),
+        out_shape=jax.ShapeDtypeStruct((z.tile, z.tile), jnp.float32),
         out_specs=VMEM,
         compiler_params=PARAMS,
         cost_estimate=z.cost(20, 1),
-        name="masks",
-    )(pattern)
+        name="unit",
+    )()
 
 
 def pack_kernel(z, margin, factor, pattern, _, near, far, cross):
@@ -193,7 +189,7 @@
         near[3 * z.cells + f // per_block, low : low + FLAG_ROWS] = value
 
 
-def pack(z, margin, factor, pattern, mask_near):
+def pack(z, margin, factor, pattern, unit):
     kind = margin.dtype
     return pl.pallas_call(
         functools.partial(pack_kernel, z),
@@ -206,11 +202,11 @@
         out_specs=(VMEM, VMEM, VMEM),
         compiler_params=PARAMS,
         name="pack",
-    )(margin, factor, pattern, mask_near)
+    )(margin, factor, pattern, unit)
 
 
 def inner_kernel(
-    z, pattern, mask_near, near, far, beside, z_cols, turned, p_part, d_part, squares, held16, held32,
+    z, pattern, unit, near, far, beside, z_cols, turned, p_part, d_part, squares, held16, held32,
     flags, s_cols, z_turned, image, d_near, d_beside, sums, sems,
 ):
     near_first, _ = half_starts(z)
@@ -267,13 +263,13 @@
             image[c - 1, y] = image_tile(y, c).astype(kind)
     d_part[0] = turned_sum(1, 1, (2,))
     d_part[1] = turned_sum(2, 1, (2, 3))
-    eye = identity(z)
+    eye = unit[...]
     total = jnp.zeros((8, z.tile), jnp.float32)
     for i in (1, 2, 3):
         value = -turned_sum(i, 2, (i - 1, i, i + 1))
         if i == 2:
             value = eye + value
-        value = (value * mask_near[i - 1].astype(jnp.float32)).astype(kind)
+        value = own_masked(z, pattern, near_first, i - 1, value).astype(kind)
         d_near[i - 1] = value
         total = total + sum_squares(z, value)
     squares[...] = total
@@ -310,7 +306,7 @@
         copy.wait()
 
 
-def inner_step(z, pattern, mask_near, near, far, beside):
+def inner_step(z, pattern, unit, near, far, beside):
     kind = near.dtype
     tile = z.tile
     return pl.pallas_call(
@@ -339,11 +335,11 @@
         compiler_params=PARAMS,
         cost_estimate=z.cost(54, 8),
         name="inner",
-    )(pattern, mask_near, near, far, beside)
+    )(pattern, unit, near, far, beside)
 
 
 def outer_kernel(
-    z, pattern, far, cross, z_cols, turned, p_part, d_part, squares, d_out, carry, spread_out, s_far,
+    z, pattern, unit, far, cross, z_cols, turned, p_part, d_part, squares, d_out, carry, spread_out, s_far,
     z_far, d_far, spread, sems,
 ):
     _, far_first = half_starts(z)
@@ -373,7 +369,7 @@
     )
     values = (
         -(dot(z_far[0].T, image[0]) + dot(z_far[1].T, image[1]) + dot(z_far[2].T, image[2])),
-        identity(z) - (dot(turned[0], image[1]) + dot(turned[1], image[2]) + d_part[0]),
+        unit[...] - (dot(turned[0], image[1]) + dot(turned[1], image[2]) + d_part[0]),
         -(dot(turned[2], image[2]) + d_part[1]),
     )
     total = squares[...]
@@ -394,7 +390,7 @@
         copy.wait()
 
 
-def outer_step(z, pattern, far, cross, z_cols, turned, p_part, d_part, squares):
+def outer_step(z, pattern, unit, far, cross, z_cols, turned, p_part, d_part, squares):
     kind = far.dtype
     return pl.pallas_call(
         functools.partial(outer_kernel, z),
@@ -403,7 +399,7 @@
             z.tiles(5, kind),
             jax.ShapeDtypeStruct((z.devices, 1, z.block), jnp.float32),
         ),
-        in_specs=[SMEM] + [VMEM] * 7,
+        in_specs=[SMEM] + [VMEM] * 8,
         out_specs=(HBM, HBM, HBM),
         scratch_shapes=[
             pltpu.VMEM((3, z.tile, z.tile), kind),
@@ -415,7 +411,7 @@
         compiler_params=PARAMS,
         cost_estimate=z.cost(9, 4),
         name="outer",
-    )(pattern, far, cross, z_cols, turned, p_part, d_part, squares)
+    )(pattern, unit, far, cross, z_cols, turned, p_part, d_part, squares)
 
 
 def middle_kernel(
@@ -590,16 +586,16 @@
     far_pairs = [(i, i + 1) for i in range(1, devices - 1, 2)]
     inner_pairs = [(i, j) for i, j in far_pairs if j % slabs]
     cross_pairs = [(i, j) for i, j in far_pairs if not j % slabs]
-    mask_near = masks(z, pattern, margin.dtype)
-    near, far, cross = pack(z, margin, factor, pattern, mask_near)
+    unit = unit_tile(z)
+    near, far, cross = pack(z, margin, factor, pattern, unit)
     beyond = lax.ppermute(far, AXES, swaps(inner_pairs))
     across = lax.ppermute(cross, AXES, swaps(cross_pairs))
     beside = lax.ppermute(near, AXES, swaps(near_pairs))
     z_cols, turned, p_part, d_part, squares, held16, held32, flags = inner_step(
-        z, pattern, mask_near, near, far, beside
+        z, pattern, unit, near, far, beside
     )
     d_out, carry, spread = outer_step(
-        z, pattern, beyond, across, z_cols, turned, p_part, d_part, squares
+        z, pattern, unit, beyond, across, z_cols, turned, p_part, d_part, squares
     )
     gathered = lax.all_to_all(spread, AXES, 0, 0, tiled=True)
     d_in = lax.ppermute(d_out, AXES, swaps(far_pairs))

time: 37.2 us -> 36.5 us (0.981)
  Pallas kernels: 13.3 us -> 12.7 us
    pallas_call x1, Pallas kernels: 0.62 us -> 0.02 us  [unit_tile(): pl.pallas_call(functools.partial(unit_kernel, z), out_shape=jax.ShapeDtyp...]
    unnamed x14 -> x12, local copies, waits for them, and re-layouts: 2.51 us -> 2.51 us
  transfers between devices with their start and end apart: 5 -> 5, of which waited for: 2 -> 2; matrix products, arithmetic and copies ran while one was open for 0% -> 0% of each run, Pallas kernels for 24% -> 25%
where the time goes in v2:
time: 36.5 us; the launch traced here: 36.3 us
  starting transfers between devices  18.1 us (50%)
  Pallas kernels  12.7 us (35%)
  local copies, waits for them, and re-layouts  2.51 us (7%)
  waiting for transfers between devices  2.27 us (6%)
  between operations  0.78 us (2%)
    all_to_all x1, starting transfers between devices, per_device(): gathered = lax.all_to_all(spread, AXES, 0, 0, tiled=True)  14.8 us
    pallas_call x1, Pallas kernels, inner_step(): pl.pallas_call(functools.partial(inner_kernel, z), out_shape=(jax.ShapeDt...  3.89 us
    pallas_call x1, Pallas kernels, last_step(): pl.pallas_call(functools.partial(last_kernel, z), out_shape=tuple((jax.Sh...  2.88 us
    unnamed x12, local copies, waits for them, and re-layouts  2.51 us
    pallas_call x1, Pallas kernels, middle_step(): pl.pallas_call(functools.partial(middle_kernel, z), out_shape=(jax.ShapeD...  2.16 us
    pallas_call x1, Pallas kernels, outer_step(): pl.pallas_call(functools.partial(outer_kernel, z), out_shape=(z.tiles(2,...  2.12 us
    all_to_all x1, waiting for transfers between devices, per_device(): gathered = lax.all_to_all(spread, AXES, 0, 0, tiled=True)  1.4 us
    ppermute x1, starting transfers between devices, per_device(): d_in = lax.ppermute(d_out, AXES, swaps(far_pairs))  1.35 us
  transfers between devices with their start and end apart: 5, of which 2 were waited for; matrix products, arithmetic and copies ran while one was open for 0% of the time, Pallas kernels for 25%

profile of v2, /device:TPU:0, one launch (start us, length us, event | category | flops | bytes accessed | tf_op | source)
XLA Modules:
  0.0 36.3 jit_solution(18253663128257956051)
XLA Ops:
  0.6 0.0 copy-start
  0.6 0.0 copy-start.1
  0.6 0.0 copy-start.3
  0.7 1.0 %copy-done = bf16[4,5,128,128]{3,2,1,0:T(8,128)(2,1)S(1)} copy-done((bf16[4,5,128,128]{3,2,1,0:T(8,128)(2,1)S(1)}, bf16[4,5,128,128]{3,2,1,0:T(8,128)(2,1)}, u32[]{:S(2)}) %copy-start) | copy-done | bytes 655384
  1.7 0.2 copy-done.1
  1.9 0.0 copy-done.3
  1.9 0.9 %pack.1 = (bf16[31,128,128]{2,1,0:T(8,128)(2,1)S(1)}, bf16[20,128,128]{2,1,0:T(8,128)(2,1)S(1)}, bf16[2,2,128,128]{3,2,1,0:T(8,128)(2,1)S(1)}) custom-call(bf16[4,5,128,128]{3,2,1,0:T(8,128)(2,1)S(1)} %copy-done, bf16[4,5,128,128]{3,2,1,0:T(8,128)(2,1)S(1)} %copy-done.1, s32[4,5]{1,0:T(4,128)S(1)} %copy-done.3, f32[256,256]{1,0:T(8,128)S(1)} %unit.1._), custom_call_target="tpu_custom_call" | custom-call | tf_op jit(solution)/shard_map/pack/pallas_call | solution.py:194
  2.9 0.5 %collective-permute-start = (bf16[31,128,128]{2,1,0:T(8,128)(2,1)S(1)}, bf16[31,128,128]{2,1,0:T(8,128)(2,1)S(1)}, u32[]{:S(2)}, u32[]{:S(2)}) collective-permute-start(bf16[31,128,128]{2,1,0:T(8,128)(2,1)S(1)} %get-tuple-element.22.near), channel_id=1, source_target_pairs={{0,1},{1,0},{2,3},{3,2},{4,5},{5,4},{6,7},{7,6},{8,9},{9,8},{10,11... | collective-permute-start | bytes 3047432 | tf_op jit(solution)/shard_map/ppermute | solution.py:593
  3.4 0.7 %collective-permute-start.1 = (bf16[20,128,128]{2,1,0:T(8,128)(2,1)S(1)}, bf16[20,128,128]{2,1,0:T(8,128)(2,1)S(1)}, u32[]{:S(2)}, u32[]{:S(2)}) collective-permute-start(bf16[20,128,128]{2,1,0:T(8,128)(2,1)S(1)} %get-tuple-element.23.far), channel_id=1, source_target_pairs={{1,2},{2,1},{3,4},{4,3},{5,6},{6,5},{9,10},{10,9},{11,12},{12,11},... | collective-permute-start | bytes 1966088 | tf_op jit(solution)/shard_map/ppermute | solution.py:591
  4.1 0.7 %collective-permute-start.2 = (bf16[2,2,128,128]{3,2,1,0:T(8,128)(2,1)S(1)}, bf16[2,2,128,128]{3,2,1,0:T(8,128)(2,1)S(1)}, u32[]{:S(2)}, u32[]{:S(2)}) collective-permute-start(bf16[2,2,128,128]{3,2,1,0:T(8,128)(2,1)S(1)} %get-tuple-element.27), channel_id=1, source_target_pairs={{7,8},{8,7},{15,16},{16,15},{23,24},{24,23}} | collective-permute-start | bytes 393224 | tf_op jit(solution)/shard_map/ppermute | solution.py:592
  4.8 0.9 %collective-permute-done.beside = bf16[31,128,128]{2,1,0:T(8,128)(2,1)S(1)} collective-permute-done((bf16[31,128,128]{2,1,0:T(8,128)(2,1)S(1)}, bf16[31,128,128]{2,1,0:T(8,128)(2,1)S(1)}, u32[]{:S(2)}, u32[]{:S(2)}) %collective-permute-start) | collective-permute-done | bytes 1015840 | tf_op jit(solution)/shard_map/ppermute | solution.py:593
  5.6 3.9 %inner.1 = (bf16[3,3,256,256]{3,2,1,0:T(8,128)(2,1)S(1)}, bf16[3,256,256]{2,1,0:T(8,128)(2,1)S(1)}, f32[2,256,256]{2,1,0:T(8,128)S(1)}, f32[2,256,256]{2,1,0:T(8...) custom-call(s32[4,5]{1,0:T(4,128)S(1)} %copy-done.3, ...), custom_call_target="tpu_custom_call" | custom-call | flops 1811939328 | bytes 8388608 | tf_op jit(solution)/shard_map/inner/pallas_call | solution.py:312
  9.5 0.0 copy-start.4
  9.5 0.0 collective-permute-done.2.cross
  9.5 0.0 collective-permute-done.1.far
  9.5 2.1 %outer.1 = (bf16[2,256,256]{2,1,0:T(8,128)(2,1)}, bf16[5,256,256]{2,1,0:T(8,128)(2,1)S(1)}, f32[32,1,128]{2,1,0:T(1,128)S(1)}) custom-call(s32[4,5]{1,0:T(4,128)S(1)} %copy-done.3, f32[256,256]{1,0:T(8,128)S(1)} %unit.1._, bf16[20,128,128]{2,1,0:T(8,128)(2,1)S(1)} %collective-permute-done.1.far, bf16[2,2,128,128]{3,2,1,0:T(8,128)(2,1)S(1)} %collective-permute-done.2.cross, ...), custom_call_target="tpu_custom_call" | custom-call | flops 301989888 | bytes 4194304 | tf_op jit(solution)/shard_map/outer/pallas_call | solution.py:395
  11.7 0.0 copy-done.4
  11.7 0.0 copy-start.2
  11.7 0.6 %copy-done.2 = f32[32,1,128]{2,1,0:T(1,128)} copy-done((f32[32,1,128]{2,1,0:T(1,128)}, f32[32,1,128]{2,1,0:T(1,128)S(1)}, u32[]{:S(2)}) %copy-start.2) | copy-done | bytes 16408
  12.3 1.4 %collective-permute-start.3 = (bf16[2,256,256]{2,1,0:T(8,128)(2,1)}, bf16[2,256,256]{2,1,0:T(8,128)(2,1)}, u32[]{:S(2)}, u32[]{:S(2)}) collective-permute-start(bf16[2,256,256]{2,1,0:T(8,128)(2,1)} %get-tuple-element.37), channel_id=1, source_target_pairs={{1,2},{2,1},{3,4},{4,3},{5,6},{6,5},{7,8},{8,7},{9,10},{10,9},{11,... | collective-permute-start | bytes 786440 | tf_op jit(solution)/shard_map/ppermute | solution.py:601
  13.6 14.8 %all-to-all-start = ((f32[32,1,128]{2,1,0:T(1,128)}), f32[32,1,128]{2,1,0:T(1,128)S(1)}, u32[]{:S(2)}, u32[]{:S(2)}) async-start(f32[32,1,128]{2,1,0:T(1,128)} %copy-done.2), calls=%async_computation | async-start | bytes 32768 | tf_op jit(solution)/shard_map/all_to_all | solution.py:600
  28.5 0.0 copy-start.5
  28.5 0.7 %copy-done.5 = s32[4,5]{1,0:T(4,128)S(1)} copy-done((s32[4,5]{1,0:T(4,128)S(1)}, s32[4,5]{1,0:T(4,128)}, u32[]{:S(2)}) %copy-start.5) | copy-done | bytes 104
  29.2 2.2 %middle.1 = (bf16[4,5,128,128]{3,2,1,0:T(8,128)(2,1)}, bf16[10,256,256]{2,1,0:T(8,128)(2,1)S(1)}, f32[6,256,256]{2,1,0:T(8,128)S(1)}, bf16[5,256,256]{2,1,0:T(8,128)(2,1)S(1)}, s32[4,5]{1,0:T(4,128)S(1)}) custom-call(s32[4,5]{1,0:T(4,128)S(1)} %copy-done.5, ...), custom_call_target="tpu_custom_call", output_to_operand_aliasing={{1}: (1, {}), {2}: (2, {}), {3}: (3, {}), {4}: (0, {})} | custom-call | flops 301989888 | bytes 6291456 | tf_op jit(solution)/shard_map/middle/pallas_call | solution.py:459
  31.3 0.0 collective-permute-done.3.d_in
  31.3 2.9 %last.1 = (bf16[4,5,128,128]{3,2,1,0:T(8,128)(2,1)}, bf16[10,256,256]{2,1,0:T(8,128)(2,1)S(1)}, bf16[5,256,256]{2,1,0:T(8,128)(2,1)S(1)}, bf16[2,256,256]{2,1,0:T(8,128)(2,1)}, s32[4,5]{1,0:T(4,128)S(1)}) custom-call(s32[4,5]{1,0:T(4,128)S(1)} %get-tuple-element.34.pattern_in, ...), custom_call_target="tpu_custom_call", output_to_operand_aliasing={{0}: (4, {}), {1}: (1, {}), {2}: (2, {}), {3}: (3, {}), {4}... | custom-call | flops 704643072 | bytes 4194304 | tf_op jit(solution)/shard_map/last/pallas_call | solution.py:536
  34.2 1.4 %all-to-all-done.gathered = f32[32,1,128]{2,1,0:T(1,128)S(1)} async-done(((f32[32,1,128]{2,1,0:T(1,128)}), f32[32,1,128]{2,1,0:T(1,128)S(1)}, u32[]{:S(2)}, u32[]{:S(2)}) %all-to-all-start) | async-done | bytes 16416 | tf_op jit(solution)/shard_map/all_to_all | solution.py:600
  35.6 0.7 %norm.1 = f32[1,128]{1,0:T(1,128)} custom-call(f32[32,1,128]{2,1,0:T(1,128)S(1)} %all-to-all-done.gathered, bf16[10,256,256]{2,1,0:T(8,128)(2,1)S(1)} %get-tuple-element.41._), custom_call_target="tpu_custom_call" | custom-call | tf_op jit(solution)/shard_map/norm/pallas_call | solution.py:565
  (1 shorter events, 0.0 us)
Async XLA Ops:
  0.6 1.1 %copy-start = (bf16[4,5,128,128]{3,2,1,0:T(8,128)(2,1)S(1)}, bf16[4,5,128,128]{3,2,1,0:T(8,128)(2,1)}, u32[]{:S(2)}) copy-start(bf16[4,5,128,128]{3,2,1,0:T(8,128)(2,1)} %margin.1) | copy-start | bytes 1966084
  0.6 1.3 %copy-start.1 = (bf16[4,5,128,128]{3,2,1,0:T(8,128)(2,1)S(1)}, bf16[4,5,128,128]{3,2,1,0:T(8,128)(2,1)}, u32[]{:S(2)}) copy-start(bf16[4,5,128,128]{3,2,1,0:T(8,128)(2,1)} %factor.1) | copy-start | bytes 1966084
  0.6 1.3 %copy-start.3 = (s32[4,5]{1,0:T(4,128)S(1)}, s32[4,5]{1,0:T(4,128)}, u32[]{:S(2)}) copy-start(s32[4,5]{1,0:T(4,128)} %pattern.5) | copy-start | bytes 244
  2.9 2.8 %collective-permute-start = (bf16[31,128,128]{2,1,0:T(8,128)(2,1)S(1)}, bf16[31,128,128]{2,1,0:T(8,128)(2,1)S(1)}, u32[]{:S(2)}, u32[]{:S(2)}) collective-permute-start(bf16[31,128,128]{2,1,0:T(8,128)(2,1)S(1)} %get-tuple-element.22.near), channel_id=1, source_target_pairs={{0,1},{1,0},{2,3},{3,2},{4,5},{5,4},{6,7},{7,6},{8,9},{9,8},{10,11... | collective-permute-start | bytes 3047432 | tf_op jit(solution)/shard_map/ppermute | solution.py:593
  3.4 6.2 %collective-permute-start.1 = (bf16[20,128,128]{2,1,0:T(8,128)(2,1)S(1)}, bf16[20,128,128]{2,1,0:T(8,128)(2,1)S(1)}, u32[]{:S(2)}, u32[]{:S(2)}) collective-permute-start(bf16[20,128,128]{2,1,0:T(8,128)(2,1)S(1)} %get-tuple-element.23.far), channel_id=1, source_target_pairs={{1,2},{2,1},{3,4},{4,3},{5,6},{6,5},{9,10},{10,9},{11,12},{12,11},... | collective-permute-start | bytes 1966088 | tf_op jit(solution)/shard_map/ppermute | solution.py:591
  4.1 5.5 %collective-permute-start.2 = (bf16[2,2,128,128]{3,2,1,0:T(8,128)(2,1)S(1)}, bf16[2,2,128,128]{3,2,1,0:T(8,128)(2,1)S(1)}, u32[]{:S(2)}, u32[]{:S(2)}) collective-permute-start(bf16[2,2,128,128]{3,2,1,0:T(8,128)(2,1)S(1)} %get-tuple-element.27), channel_id=1, source_target_pairs={{7,8},{8,7},{15,16},{16,15},{23,24},{24,23}} | collective-permute-start | bytes 393224 | tf_op jit(solution)/shard_map/ppermute | solution.py:592
  9.5 2.2 %copy-start.4 = (s32[4,5]{1,0:T(4,128)}, s32[4,5]{1,0:T(4,128)S(1)}, u32[]{:S(2)}) copy-start(s32[4,5]{1,0:T(4,128)S(1)} %get-tuple-element.24.pattern_in) | copy-start | bytes 244
  11.7 0.6 %copy-start.2 = (f32[32,1,128]{2,1,0:T(1,128)}, f32[32,1,128]{2,1,0:T(1,128)S(1)}, u32[]{:S(2)}) copy-start(f32[32,1,128]{2,1,0:T(1,128)S(1)} %get-tuple-element.40) | copy-start | bytes 49156
  12.3 19.0 %collective-permute-start.3 = (bf16[2,256,256]{2,1,0:T(8,128)(2,1)}, bf16[2,256,256]{2,1,0:T(8,128)(2,1)}, u32[]{:S(2)}, u32[]{:S(2)}) collective-permute-start(bf16[2,256,256]{2,1,0:T(8,128)(2,1)} %get-tuple-element.37), channel_id=1, source_target_pairs={{1,2},{2,1},{3,4},{4,3},{5,6},{6,5},{7,8},{8,7},{9,10},{10,9},{11,... | collective-permute-start | bytes 786440 | tf_op jit(solution)/shard_map/ppermute | solution.py:601
  13.6 22.0 %all-to-all-start = ((f32[32,1,128]{2,1,0:T(1,128)}), f32[32,1,128]{2,1,0:T(1,128)S(1)}, u32[]{:S(2)}, u32[]{:S(2)}) async-start(f32[32,1,128]{2,1,0:T(1,128)} %copy-done.2), calls=%async_computation | async-start | bytes 32768 | tf_op jit(solution)/shard_map/all_to_all | solution.py:600
  28.5 0.7 %copy-start.5 = (s32[4,5]{1,0:T(4,128)S(1)}, s32[4,5]{1,0:T(4,128)}, u32[]{:S(2)}) copy-start(s32[4,5]{1,0:T(4,128)} %copy-done.4) | copy-start | bytes 244

commit v3 on v2

--- a/solution.py
+++ b/solution.py
@@ -339,8 +339,8 @@
 
 
 def outer_kernel(
-    z, pattern, unit, far, cross, z_cols, turned, p_part, d_part, squares, d_out, carry, spread_out, s_far,
-    z_far, d_far, spread, sems,
+    z, pattern, unit, far, cross, z_cols, turned, p_part, d_part, squares, d_out, carry, spread, s_far,
+    z_far, d_pair, sem,
 ):
     _, far_first = half_starts(z)
     kind = far.dtype
@@ -354,13 +354,9 @@
 
     expand(z, s_far, lambda t, o: far[t * z.offsets + o])
     expand(z, z_far, factor_cell)
-    copies = []
-
-    def send(source, target):
-        copies.append(pltpu.make_async_copy(source, target, sems.at[len(copies)]))
-        copies[-1].start()
-
-    send(z_far.at[pl.ds(1, 2)], carry.at[pl.ds(0, 2)])
+    carry[0] = z_far[1]
+    carry[1] = z_far[2]
+    copy = pltpu.make_async_copy(d_pair, d_out, sem)
     link = z_cols[0, 0]
     image = (
         dot(s_far[0], link).astype(kind),
@@ -375,19 +371,18 @@
     total = squares[...]
     for e, value in enumerate(values):
         value = own_masked(z, pattern, far_first, e, value).astype(kind)
-        d_far[e] = value
+        carry[2 + e] = value
+        if e < 2:
+            d_pair[e] = value
+        if e == 1:
+            copy.start()
         total = total + sum_squares(z, value)
-        if e == 1:
-            send(d_far.at[pl.ds(0, 2)], d_out)
-    send(d_far, carry.at[pl.ds(2, 3)])
     lanes = jnp.sum(total, axis=0, keepdims=True)
     folded = lanes[:, : z.block]
     for t in range(1, z.half):
         folded = folded + lanes[:, t * z.block : (t + 1) * z.block]
     spread[...] = jnp.broadcast_to(folded[None], spread.shape)
-    send(spread, spread_out)
-    for copy in copies:
-        copy.wait()
+    copy.wait()
 
 
 def outer_step(z, pattern, unit, far, cross, z_cols, turned, p_part, d_part, squares):
@@ -400,13 +395,12 @@
             jax.ShapeDtypeStruct((z.devices, 1, z.block), jnp.float32),
         ),
         in_specs=[SMEM] + [VMEM] * 8,
-        out_specs=(HBM, HBM, HBM),
+        out_specs=(HBM, VMEM, VMEM),
         scratch_shapes=[
             pltpu.VMEM((3, z.tile, z.tile), kind),
             pltpu.VMEM((3, z.tile, z.tile), kind),
-            pltpu.VMEM((3, z.tile, z.tile), kind),
-            pltpu.VMEM((z.devices, 1, z.block), jnp.float32),
-            pltpu.SemaphoreType.DMA((4,)),
+            pltpu.VMEM((2, z.tile, z.tile), kind),
+            pltpu.SemaphoreType.DMA(()),
         ],
         compiler_params=PARAMS,
         cost_estimate=z.cost(9, 4),

time: 36.5 us -> 36.4 us (level)
  no operation moved by 1% of the time
where the time goes in v3:
time: 36.4 us; the launch traced here: 36.2 us
  starting transfers between devices  18.1 us (50%)
  Pallas kernels  12.6 us (35%)
  local copies, waits for them, and re-layouts  2.51 us (7%)
  waiting for transfers between devices  2.27 us (6%)
  between operations  0.78 us (2%)
    all_to_all x1, starting transfers between devices, per_device(): gathered = lax.all_to_all(spread, AXES, 0, 0, tiled=True)  14.8 us
    pallas_call x1, Pallas kernels, inner_step(): pl.pallas_call(functools.partial(inner_kernel, z), out_shape=(jax.ShapeDt...  3.89 us
    pallas_call x1, Pallas kernels, last_step(): pl.pallas_call(functools.partial(last_kernel, z), out_shape=tuple((jax.Sh...  2.88 us
    unnamed x12, local copies, waits for them, and re-layouts  2.51 us
    pallas_call x1, Pallas kernels, middle_step(): pl.pallas_call(functools.partial(middle_kernel, z), out_shape=(jax.ShapeD...  2.16 us
    pallas_call x1, Pallas kernels, outer_step(): pl.pallas_call(functools.partial(outer_kernel, z), out_shape=(z.tiles(2,...  2.02 us
    all_to_all x1, waiting for transfers between devices, per_device(): gathered = lax.all_to_all(spread, AXES, 0, 0, tiled=True)  1.39 us
    ppermute x1, starting transfers between devices, per_device(): d_in = lax.ppermute(d_out, AXES, swaps(far_pairs))  1.35 us
  transfers between devices with their start and end apart: 5, of which 2 were waited for; matrix products, arithmetic and copies ran while one was open for 0% of the time, Pallas kernels for 25%

profile of v3, /device:TPU:0, one launch (start us, length us, event | category | flops | bytes accessed | tf_op | source)
XLA Modules:
  0.0 36.2 jit_solution(6320260849412894311)
XLA Ops:
  0.6 0.0 copy-start
  0.6 0.0 copy-start.1
  0.6 0.0 copy-start.3
  0.7 1.0 %copy-done = bf16[4,5,128,128]{3,2,1,0:T(8,128)(2,1)S(1)} copy-done((bf16[4,5,128,128]{3,2,1,0:T(8,128)(2,1)S(1)}, bf16[4,5,128,128]{3,2,1,0:T(8,128)(2,1)}, u32[]{:S(2)}) %copy-start) | copy-done | bytes 655384
  1.7 0.2 copy-done.1
  1.9 0.0 copy-done.3
  1.9 0.9 %pack.1 = (bf16[31,128,128]{2,1,0:T(8,128)(2,1)S(1)}, bf16[20,128,128]{2,1,0:T(8,128)(2,1)S(1)}, bf16[2,2,128,128]{3,2,1,0:T(8,128)(2,1)S(1)}) custom-call(bf16[4,5,128,128]{3,2,1,0:T(8,128)(2,1)S(1)} %copy-done, bf16[4,5,128,128]{3,2,1,0:T(8,128)(2,1)S(1)} %copy-done.1, s32[4,5]{1,0:T(4,128)S(1)} %copy-done.3, f32[256,256]{1,0:T(8,128)S(1)} %unit.1._), custom_call_target="tpu_custom_call" | custom-call | tf_op jit(solution)/shard_map/pack/pallas_call | solution.py:194
  2.9 0.5 %collective-permute-start = (bf16[31,128,128]{2,1,0:T(8,128)(2,1)S(1)}, bf16[31,128,128]{2,1,0:T(8,128)(2,1)S(1)}, u32[]{:S(2)}, u32[]{:S(2)}) collective-permute-start(bf16[31,128,128]{2,1,0:T(8,128)(2,1)S(1)} %get-tuple-element.22.near), channel_id=1, source_target_pairs={{0,1},{1,0},{2,3},{3,2},{4,5},{5,4},{6,7},{7,6},{8,9},{9,8},{10,11... | collective-permute-start | bytes 3047432 | tf_op jit(solution)/shard_map/ppermute | solution.py:587
  3.4 0.7 %collective-permute-start.1 = (bf16[20,128,128]{2,1,0:T(8,128)(2,1)S(1)}, bf16[20,128,128]{2,1,0:T(8,128)(2,1)S(1)}, u32[]{:S(2)}, u32[]{:S(2)}) collective-permute-start(bf16[20,128,128]{2,1,0:T(8,128)(2,1)S(1)} %get-tuple-element.23.far), channel_id=1, source_target_pairs={{1,2},{2,1},{3,4},{4,3},{5,6},{6,5},{9,10},{10,9},{11,12},{12,11},... | collective-permute-start | bytes 1966088 | tf_op jit(solution)/shard_map/ppermute | solution.py:585
  4.1 0.7 %collective-permute-start.2 = (bf16[2,2,128,128]{3,2,1,0:T(8,128)(2,1)S(1)}, bf16[2,2,128,128]{3,2,1,0:T(8,128)(2,1)S(1)}, u32[]{:S(2)}, u32[]{:S(2)}) collective-permute-start(bf16[2,2,128,128]{3,2,1,0:T(8,128)(2,1)S(1)} %get-tuple-element.27), channel_id=1, source_target_pairs={{7,8},{8,7},{15,16},{16,15},{23,24},{24,23}} | collective-permute-start | bytes 393224 | tf_op jit(solution)/shard_map/ppermute | solution.py:586
  4.8 0.9 %collective-permute-done.beside = bf16[31,128,128]{2,1,0:T(8,128)(2,1)S(1)} collective-permute-done((bf16[31,128,128]{2,1,0:T(8,128)(2,1)S(1)}, bf16[31,128,128]{2,1,0:T(8,128)(2,1)S(1)}, u32[]{:S(2)}, u32[]{:S(2)}) %collective-permute-start) | collective-permute-done | bytes 1015840 | tf_op jit(solution)/shard_map/ppermute | solution.py:587
  5.6 3.9 %inner.1 = (bf16[3,3,256,256]{3,2,1,0:T(8,128)(2,1)S(1)}, bf16[3,256,256]{2,1,0:T(8,128)(2,1)S(1)}, f32[2,256,256]{2,1,0:T(8,128)S(1)}, f32[2,256,256]{2,1,0:T(8...) custom-call(s32[4,5]{1,0:T(4,128)S(1)} %copy-done.3, ...), custom_call_target="tpu_custom_call" | custom-call | flops 1811939328 | bytes 8388608 | tf_op jit(solution)/shard_map/inner/pallas_call | solution.py:312
  9.5 0.0 copy-start.4
  9.5 0.0 collective-permute-done.2.cross
  9.5 0.0 collective-permute-done.1.far
  9.5 2.0 %outer.1 = (bf16[2,256,256]{2,1,0:T(8,128)(2,1)}, bf16[5,256,256]{2,1,0:T(8,128)(2,1)S(1)}, f32[32,1,128]{2,1,0:T(1,128)S(1)}) custom-call(s32[4,5]{1,0:T(4,128)S(1)} %copy-done.3, f32[256,256]{1,0:T(8,128)S(1)} %unit.1._, bf16[20,128,128]{2,1,0:T(8,128)(2,1)S(1)} %collective-permute-done.1.far, bf16[2,2,128,128]{3,2,1,0:T(8,128)(2,1)S(1)} %collective-permute-done.2.cross, ...), custom_call_target="tpu_custom_call" | custom-call | flops 301989888 | bytes 4194304 | tf_op jit(solution)/shard_map/outer/pallas_call | solution.py:390
  11.6 0.0 copy-done.4
  11.6 0.0 copy-start.2
  11.6 0.6 %copy-done.2 = f32[32,1,128]{2,1,0:T(1,128)} copy-done((f32[32,1,128]{2,1,0:T(1,128)}, f32[32,1,128]{2,1,0:T(1,128)S(1)}, u32[]{:S(2)}) %copy-start.2) | copy-done | bytes 16408
  12.2 1.4 %collective-permute-start.3 = (bf16[2,256,256]{2,1,0:T(8,128)(2,1)}, bf16[2,256,256]{2,1,0:T(8,128)(2,1)}, u32[]{:S(2)}, u32[]{:S(2)}) collective-permute-start(bf16[2,256,256]{2,1,0:T(8,128)(2,1)} %get-tuple-element.37), channel_id=1, source_target_pairs={{1,2},{2,1},{3,4},{4,3},{5,6},{6,5},{7,8},{8,7},{9,10},{10,9},{11,... | collective-permute-start | bytes 786440 | tf_op jit(solution)/shard_map/ppermute | solution.py:595
  13.5 14.8 %all-to-all-start = ((f32[32,1,128]{2,1,0:T(1,128)}), f32[32,1,128]{2,1,0:T(1,128)S(1)}, u32[]{:S(2)}, u32[]{:S(2)}) async-start(f32[32,1,128]{2,1,0:T(1,128)} %copy-done.2), calls=%async_computation | async-start | bytes 32768 | tf_op jit(solution)/shard_map/all_to_all | solution.py:594
  28.4 0.0 copy-start.5
  28.4 0.7 %copy-done.5 = s32[4,5]{1,0:T(4,128)S(1)} copy-done((s32[4,5]{1,0:T(4,128)S(1)}, s32[4,5]{1,0:T(4,128)}, u32[]{:S(2)}) %copy-start.5) | copy-done | bytes 104
  29.1 2.2 %middle.1 = (bf16[4,5,128,128]{3,2,1,0:T(8,128)(2,1)}, bf16[10,256,256]{2,1,0:T(8,128)(2,1)S(1)}, f32[6,256,256]{2,1,0:T(8,128)S(1)}, bf16[5,256,256]{2,1,0:T(8,128)(2,1)S(1)}, s32[4,5]{1,0:T(4,128)S(1)}) custom-call(s32[4,5]{1,0:T(4,128)S(1)} %copy-done.5, ...), custom_call_target="tpu_custom_call", output_to_operand_aliasing={{1}: (1, {}), {2}: (2, {}), {3}: (3, {}), {4}: (0, {})} | custom-call | flops 301989888 | bytes 6291456 | tf_op jit(solution)/shard_map/middle/pallas_call | solution.py:453
  31.2 0.0 collective-permute-done.3.d_in
  31.2 2.9 %last.1 = (bf16[4,5,128,128]{3,2,1,0:T(8,128)(2,1)}, bf16[10,256,256]{2,1,0:T(8,128)(2,1)S(1)}, bf16[5,256,256]{2,1,0:T(8,128)(2,1)S(1)}, bf16[2,256,256]{2,1,0:T(8,128)(2,1)}, s32[4,5]{1,0:T(4,128)S(1)}) custom-call(s32[4,5]{1,0:T(4,128)S(1)} %get-tuple-element.34.pattern_in, ...), custom_call_target="tpu_custom_call", output_to_operand_aliasing={{0}: (4, {}), {1}: (1, {}), {2}: (2, {}), {3}: (3, {}), {4}... | custom-call | flops 704643072 | bytes 4194304 | tf_op jit(solution)/shard_map/last/pallas_call | solution.py:530
  34.1 1.4 %all-to-all-done.gathered = f32[32,1,128]{2,1,0:T(1,128)S(1)} async-done(((f32[32,1,128]{2,1,0:T(1,128)}), f32[32,1,128]{2,1,0:T(1,128)S(1)}, u32[]{:S(2)}, u32[]{:S(2)}) %all-to-all-start) | async-done | bytes 16416 | tf_op jit(solution)/shard_map/all_to_all | solution.py:594
  35.5 0.7 %norm.1 = f32[1,128]{1,0:T(1,128)} custom-call(f32[32,1,128]{2,1,0:T(1,128)S(1)} %all-to-all-done.gathered, bf16[10,256,256]{2,1,0:T(8,128)(2,1)S(1)} %get-tuple-element.41._), custom_call_target="tpu_custom_call" | custom-call | tf_op jit(solution)/shard_map/norm/pallas_call | solution.py:559
  (1 shorter events, 0.0 us)
Async XLA Ops:
  0.6 1.1 %copy-start = (bf16[4,5,128,128]{3,2,1,0:T(8,128)(2,1)S(1)}, bf16[4,5,128,128]{3,2,1,0:T(8,128)(2,1)}, u32[]{:S(2)}) copy-start(bf16[4,5,128,128]{3,2,1,0:T(8,128)(2,1)} %margin.1) | copy-start | bytes 1966084
  0.6 1.3 %copy-start.1 = (bf16[4,5,128,128]{3,2,1,0:T(8,128)(2,1)S(1)}, bf16[4,5,128,128]{3,2,1,0:T(8,128)(2,1)}, u32[]{:S(2)}) copy-start(bf16[4,5,128,128]{3,2,1,0:T(8,128)(2,1)} %factor.1) | copy-start | bytes 1966084
  0.6 1.3 %copy-start.3 = (s32[4,5]{1,0:T(4,128)S(1)}, s32[4,5]{1,0:T(4,128)}, u32[]{:S(2)}) copy-start(s32[4,5]{1,0:T(4,128)} %pattern.5) | copy-start | bytes 244
  2.9 2.8 %collective-permute-start = (bf16[31,128,128]{2,1,0:T(8,128)(2,1)S(1)}, bf16[31,128,128]{2,1,0:T(8,128)(2,1)S(1)}, u32[]{:S(2)}, u32[]{:S(2)}) collective-permute-start(bf16[31,128,128]{2,1,0:T(8,128)(2,1)S(1)} %get-tuple-element.22.near), channel_id=1, source_target_pairs={{0,1},{1,0},{2,3},{3,2},{4,5},{5,4},{6,7},{7,6},{8,9},{9,8},{10,11... | collective-permute-start | bytes 3047432 | tf_op jit(solution)/shard_map/ppermute | solution.py:587
  3.4 6.2 %collective-permute-start.1 = (bf16[20,128,128]{2,1,0:T(8,128)(2,1)S(1)}, bf16[20,128,128]{2,1,0:T(8,128)(2,1)S(1)}, u32[]{:S(2)}, u32[]{:S(2)}) collective-permute-start(bf16[20,128,128]{2,1,0:T(8,128)(2,1)S(1)} %get-tuple-element.23.far), channel_id=1, source_target_pairs={{1,2},{2,1},{3,4},{4,3},{5,6},{6,5},{9,10},{10,9},{11,12},{12,11},... | collective-permute-start | bytes 1966088 | tf_op jit(solution)/shard_map/ppermute | solution.py:585
  4.1 5.5 %collective-permute-start.2 = (bf16[2,2,128,128]{3,2,1,0:T(8,128)(2,1)S(1)}, bf16[2,2,128,128]{3,2,1,0:T(8,128)(2,1)S(1)}, u32[]{:S(2)}, u32[]{:S(2)}) collective-permute-start(bf16[2,2,128,128]{3,2,1,0:T(8,128)(2,1)S(1)} %get-tuple-element.27), channel_id=1, source_target_pairs={{7,8},{8,7},{15,16},{16,15},{23,24},{24,23}} | collective-permute-start | bytes 393224 | tf_op jit(solution)/shard_map/ppermute | solution.py:586
  9.5 2.1 %copy-start.4 = (s32[4,5]{1,0:T(4,128)}, s32[4,5]{1,0:T(4,128)S(1)}, u32[]{:S(2)}) copy-start(s32[4,5]{1,0:T(4,128)S(1)} %get-tuple-element.24.pattern_in) | copy-start | bytes 244
  11.6 0.6 %copy-start.2 = (f32[32,1,128]{2,1,0:T(1,128)}, f32[32,1,128]{2,1,0:T(1,128)S(1)}, u32[]{:S(2)}) copy-start(f32[32,1,128]{2,1,0:T(1,128)S(1)} %get-tuple-element.40) | copy-start | bytes 49156
  12.2 19.0 %collective-permute-start.3 = (bf16[2,256,256]{2,1,0:T(8,128)(2,1)}, bf16[2,256,256]{2,1,0:T(8,128)(2,1)}, u32[]{:S(2)}, u32[]{:S(2)}) collective-permute-start(bf16[2,256,256]{2,1,0:T(8,128)(2,1)} %get-tuple-element.37), channel_id=1, source_target_pairs={{1,2},{2,1},{3,4},{4,3},{5,6},{6,5},{7,8},{8,7},{9,10},{10,9},{11,... | collective-permute-start | bytes 786440 | tf_op jit(solution)/shard_map/ppermute | solution.py:595
  13.5 22.0 %all-to-all-start = ((f32[32,1,128]{2,1,0:T(1,128)}), f32[32,1,128]{2,1,0:T(1,128)S(1)}, u32[]{:S(2)}, u32[]{:S(2)}) async-start(f32[32,1,128]{2,1,0:T(1,128)} %copy-done.2), calls=%async_computation | async-start | bytes 32768 | tf_op jit(solution)/shard_map/all_to_all | solution.py:594
  28.4 0.7 %copy-start.5 = (s32[4,5]{1,0:T(4,128)S(1)}, s32[4,5]{1,0:T(4,128)}, u32[]{:S(2)}) copy-start(s32[4,5]{1,0:T(4,128)} %copy-done.4) | copy-start | bytes 244

commit v4 on v3

--- a/solution.py
+++ b/solution.py
@@ -155,7 +155,7 @@
     )()
 
 
-def pack_kernel(z, margin, factor, pattern, _, near, far, cross):
+def pack_kernel(z, margin, factor, pattern, _, near, far_s, far_z, cross):
     near_first, far_first = half_starts(z)
     first_row = lax.axis_index("slab") * z.columns
     plan = ((margin, far_first), (factor, far_first), (margin, near_first), (factor, near_first))
@@ -171,10 +171,10 @@
                 cell = t * z.offsets + o
                 u = o + t - z.half
                 if k == 0:
-                    far[cell] = value
+                    far_s[cell] = value
                     near[2 * z.cells + cell] = value
                 elif k == 1:
-                    far[z.cells + cell] = value
+                    far_z[cell] = value
                     if 0 <= u < z.half:
                         cross[t, u] = value
                 else:
@@ -195,18 +195,19 @@
         functools.partial(pack_kernel, z),
         out_shape=(
             jax.ShapeDtypeStruct((3 * z.cells + z.flag_blocks, z.block, z.block), kind),
-            jax.ShapeDtypeStruct((2 * z.cells, z.block, z.block), kind),
+            jax.ShapeDtypeStruct((z.cells, z.block, z.block), kind),
+            jax.ShapeDtypeStruct((z.cells, z.block, z.block), kind),
             jax.ShapeDtypeStruct((z.half, z.half, z.block, z.block), kind),
         ),
         in_specs=[VMEM, VMEM, SMEM, VMEM],
-        out_specs=(VMEM, VMEM, VMEM),
+        out_specs=(VMEM,) * 4,
         compiler_params=PARAMS,
         name="pack",
     )(margin, factor, pattern, unit)
 
 
 def inner_kernel(
-    z, pattern, unit, near, far, beside, z_cols, turned, p_part, d_part, squares, held16, held32,
+    z, pattern, unit, near, far_s, far_z, beside, z_cols, turned, p_part, d_part, squares, held16, held32,
     flags, s_cols, z_turned, image, d_near, d_beside, sums, sems,
 ):
     near_first, _ = half_starts(z)
@@ -215,11 +216,11 @@
     def cells_of(ref, base):
         return lambda t, o: ref[base + t * z.offsets + o]
 
-    expand(z, s_cols.at[0], cells_of(far, 0))
+    expand(z, s_cols.at[0], cells_of(far_s, 0))
     expand(z, s_cols.at[1], cells_of(near, 0))
     expand(z, s_cols.at[2], cells_of(beside, 0))
     expand(z, s_cols.at[3], cells_of(beside, 2 * z.cells))
-    expand(z, z_cols.at[0], cells_of(far, z.cells))
+    expand(z, z_cols.at[0], cells_of(far_z, 0))
     expand(z, z_cols.at[1], cells_of(near, z.cells))
     expand(z, z_cols.at[2], cells_of(beside, z.cells))
     moves = [
@@ -306,7 +307,7 @@
         copy.wait()
 
 
-def inner_step(z, pattern, unit, near, far, beside):
+def inner_step(z, pattern, unit, near, far_s, far_z, beside):
     kind = near.dtype
     tile = z.tile
     return pl.pallas_call(
@@ -321,7 +322,7 @@
             z.tiles(6, jnp.float32),
             jax.ShapeDtypeStruct(pattern.shape, pattern.dtype),
         ),
-        in_specs=[SMEM, VMEM, VMEM, VMEM, VMEM],
+        in_specs=[SMEM] + [VMEM] * 5,
         out_specs=(VMEM,) * 5 + (HBM,) * 3,
         scratch_shapes=[
             pltpu.VMEM((4, 3, tile, tile), kind),
@@ -335,18 +336,18 @@
         compiler_params=PARAMS,
         cost_estimate=z.cost(54, 8),
         name="inner",
-    )(pattern, unit, near, far, beside)
+    )(pattern, unit, near, far_s, far_z, beside)
 
 
 def outer_kernel(
-    z, pattern, unit, far, cross, z_cols, turned, p_part, d_part, squares, d_out, carry, spread, s_far,
+    z, pattern, unit, far, far_z, cross, z_cols, turned, p_part, d_part, squares, d_out, carry, spread, s_far,
     z_far, d_pair, sem,
 ):
     _, far_first = half_starts(z)
     kind = far.dtype
 
     def factor_cell(t, o):
-        value = far[z.cells + t * z.offsets + o]
+        value = far_z[t * z.offsets + o]
         u = o + t - z.half
         if 0 <= u < z.half:
             value = value + cross[t, u]
@@ -385,7 +386,7 @@
     copy.wait()
 
 
-def outer_step(z, pattern, unit, far, cross, z_cols, turned, p_part, d_part, squares):
+def outer_step(z, pattern, unit, far, far_z, cross, z_cols, turned, p_part, d_part, squares):
     kind = far.dtype
     return pl.pallas_call(
         functools.partial(outer_kernel, z),
@@ -394,7 +395,7 @@
             z.tiles(5, kind),
             jax.ShapeDtypeStruct((z.devices, 1, z.block), jnp.float32),
         ),
-        in_specs=[SMEM] + [VMEM] * 8,
+        in_specs=[SMEM] + [VMEM] * 9,
         out_specs=(HBM, VMEM, VMEM),
         scratch_shapes=[
             pltpu.VMEM((3, z.tile, z.tile), kind),
@@ -405,7 +406,7 @@
         compiler_params=PARAMS,
         cost_estimate=z.cost(9, 4),
         name="outer",
-    )(pattern, unit, far, cross, z_cols, turned, p_part, d_part, squares)
+    )(pattern, unit, far, far_z, cross, z_cols, turned, p_part, d_part, squares)
 
 
 def middle_kernel(
@@ -581,15 +582,16 @@
     inner_pairs = [(i, j) for i, j in far_pairs if j % slabs]
     cross_pairs = [(i, j) for i, j in far_pairs if not j % slabs]
     unit = unit_tile(z)
-    near, far, cross = pack(z, margin, factor, pattern, unit)
-    beyond = lax.ppermute(far, AXES, swaps(inner_pairs))
+    near, far_s, far_z, cross = pack(z, margin, factor, pattern, unit)
+    beyond_s = lax.ppermute(far_s, AXES, swaps(inner_pairs))
+    beyond_z = lax.ppermute(far_z, AXES, swaps(inner_pairs))
     across = lax.ppermute(cross, AXES, swaps(cross_pairs))
     beside = lax.ppermute(near, AXES, swaps(near_pairs))
     z_cols, turned, p_part, d_part, squares, held16, held32, flags = inner_step(
-        z, pattern, unit, near, far, beside
+        z, pattern, unit, near, far_s, far_z, beside
     )
     d_out, carry, spread = outer_step(
-        z, pattern, unit, beyond, across, z_cols, turned, p_part, d_part, squares
+        z, pattern, unit, beyond_s, beyond_z, across, z_cols, turned, p_part, d_part, squares
     )
     gathered = lax.all_to_all(spread, AXES, 0, 0, tiled=True)
     d_in = lax.ppermute(d_out, AXES, swaps(far_pairs))

time: 36.4 us -> 36.5 us (level)
  waiting for transfers between devices: 2.27 us -> 1.6 us
  starting transfers between devices: 18.1 us -> 18.7 us
    ppermute x1, waiting for transfers between devices: 0.86 us -> 0.2 us  [per_device(): beside = lax.ppermute(near, AXES, swaps(near_pairs))]
    ppermute x1 -> x2, starting transfers between devices: 0.69 us -> 1.35 us  [the longest x1 0.68 us: per_device(): beyond_z = lax.ppermute(far_z, AXES, swaps(inner_pairs))]
  transfers between devices with their start and end apart: 5 -> 6, of which waited for: 2 -> 2; matrix products, arithmetic and copies ran while one was open for 0% -> 0% of each run, Pallas kernels for 25% -> 25%
where the time goes in v4:
time: 36.5 us; the launch traced here: 36.2 us
  starting transfers between devices  18.7 us (51%)
  Pallas kernels  12.6 us (35%)
  local copies, waits for them, and re-layouts  2.51 us (7%)
  waiting for transfers between devices  1.6 us (4%)
  between operations  0.8 us (2%)
    all_to_all x1, starting transfers between devices, per_device(): gathered = lax.all_to_all(spread, AXES, 0, 0, tiled=True)  14.8 us
    pallas_call x1, Pallas kernels, inner_step(): pl.pallas_call(functools.partial(inner_kernel, z), out_shape=(jax.ShapeDt...  3.89 us
    pallas_call x1, Pallas kernels, last_step(): pl.pallas_call(functools.partial(last_kernel, z), out_shape=tuple((jax.Sh...  2.88 us
    unnamed x12, local copies, waits for them, and re-layouts  2.51 us
    pallas_call x1, Pallas kernels, middle_step(): pl.pallas_call(functools.partial(middle_kernel, z), out_shape=(jax.ShapeD...  2.16 us
    pallas_call x1, Pallas kernels, outer_step(): pl.pallas_call(functools.partial(outer_kernel, z), out_shape=(z.tiles(2,...  2.01 us
    all_to_all x1, waiting for transfers between devices, per_device(): gathered = lax.all_to_all(spread, AXES, 0, 0, tiled=True)  1.39 us
    ppermute x1, starting transfers between devices, per_device(): d_in = lax.ppermute(d_out, AXES, swaps(far_pairs))  1.35 us
  transfers between devices with their start and end apart: 6, of which 2 were waited for; matrix products, arithmetic and copies ran while one was open for 0% of the time, Pallas kernels for 25%

profile of v4, /device:TPU:0, one launch (start us, length us, event | category | flops | bytes accessed | tf_op | source)
XLA Modules:
  0.0 36.2 jit_solution(17402612171226270761)
XLA Ops:
  0.6 0.0 copy-start
  0.6 0.0 copy-start.1
  0.6 0.0 copy-start.3
  0.7 1.0 %copy-done = bf16[4,5,128,128]{3,2,1,0:T(8,128)(2,1)S(1)} copy-done((bf16[4,5,128,128]{3,2,1,0:T(8,128)(2,1)S(1)}, bf16[4,5,128,128]{3,2,1,0:T(8,128)(2,1)}, u32[]{:S(2)}) %copy-start) | copy-done | bytes 655384
  1.7 0.2 copy-done.1
  1.9 0.0 copy-done.3
  1.9 0.9 %pack.1 = (bf16[31,128,128]{2,1,0:T(8,128)(2,1)S(1)}, bf16[10,128,128]{2,1,0:T(8,128)(2,1)S(1)}, bf16[10,128,128]{2,1,0:T(8,128)(2,1)S(1)}, bf16[2,2,128,128]{3,2,1,0:T(8,128)(2,1)S(1)}) custom-call(bf16[4,5,128,128]{3,2,1,0:T(8,128)(2,1)S(1)} %copy-done, bf16[4,5,128,128]{3,2,1,0:T(8,128)(2,1)S(1)} %copy-done.1, s32[4,5]{1,0:T(4,128)S(1)} %copy-done.3, ...), custom_call_target="tpu_custom_call" | custom-call | tf_op jit(solution)/shard_map/pack/pallas_call | solution.py:194
  2.9 0.5 %collective-permute-start = (bf16[31,128,128]{2,1,0:T(8,128)(2,1)S(1)}, bf16[31,128,128]{2,1,0:T(8,128)(2,1)S(1)}, u32[]{:S(2)}, u32[]{:S(2)}) collective-permute-start(bf16[31,128,128]{2,1,0:T(8,128)(2,1)S(1)} %get-tuple-element.23.near), channel_id=1, source_target_pairs={{0,1},{1,0},{2,3},{3,2},{4,5},{5,4},{6,7},{7,6},{8,9},{9,8},{10,11... | collective-permute-start | bytes 3047432 | tf_op jit(solution)/shard_map/ppermute | solution.py:589
  3.4 0.7 %collective-permute-start.1 = (bf16[10,128,128]{2,1,0:T(8,128)(2,1)S(1)}, bf16[10,128,128]{2,1,0:T(8,128)(2,1)S(1)}, u32[]{:S(2)}, u32[]{:S(2)}) collective-permute-start(bf16[10,128,128]{2,1,0:T(8,128)(2,1)S(1)} %get-tuple-element.24.far_s), channel_id=1, source_target_pairs={{1,2},{2,1},{3,4},{4,3},{5,6},{6,5},{9,10},{10,9},{11,12},{12,11},... | collective-permute-start | bytes 983048 | tf_op jit(solution)/shard_map/ppermute | solution.py:586
  4.1 0.7 %collective-permute-start.2 = (bf16[10,128,128]{2,1,0:T(8,128)(2,1)S(1)}, bf16[10,128,128]{2,1,0:T(8,128)(2,1)S(1)}, u32[]{:S(2)}, u32[]{:S(2)}) collective-permute-start(bf16[10,128,128]{2,1,0:T(8,128)(2,1)S(1)} %get-tuple-element.25.far_z), channel_id=1, source_target_pairs={{1,2},{2,1},{3,4},{4,3},{5,6},{6,5},{9,10},{10,9},{11,12},{12,11},... | collective-permute-start | bytes 983048 | tf_op jit(solution)/shard_map/ppermute | solution.py:587
  4.7 0.7 %collective-permute-start.3 = (bf16[2,2,128,128]{3,2,1,0:T(8,128)(2,1)S(1)}, bf16[2,2,128,128]{3,2,1,0:T(8,128)(2,1)S(1)}, u32[]{:S(2)}, u32[]{:S(2)}) collective-permute-start(bf16[2,2,128,128]{3,2,1,0:T(8,128)(2,1)S(1)} %get-tuple-element.29), channel_id=1, source_target_pairs={{7,8},{8,7},{15,16},{16,15},{23,24},{24,23}} | collective-permute-start | bytes 393224 | tf_op jit(solution)/shard_map/ppermute | solution.py:588
  5.4 0.2 collective-permute-done.beside
  5.6 3.9 %inner.1 = (bf16[3,3,256,256]{3,2,1,0:T(8,128)(2,1)S(1)}, bf16[3,256,256]{2,1,0:T(8,128)(2,1)S(1)}, f32[2,256,256]{2,1,0:T(8,128)S(1)}, f32[2,256,256]{2,1,0:T(8...) custom-call(s32[4,5]{1,0:T(4,128)S(1)} %copy-done.3, ...), custom_call_target="tpu_custom_call" | custom-call | flops 1811939328 | bytes 8388608 | tf_op jit(solution)/shard_map/inner/pallas_call | solution.py:313
  9.5 0.0 copy-start.4
  9.5 0.0 collective-permute-done.3.cross
  9.5 0.0 collective-permute-done.1.far
  9.5 0.0 collective-permute-done.2.far_z
  9.6 2.0 %outer.1 = (bf16[2,256,256]{2,1,0:T(8,128)(2,1)}, bf16[5,256,256]{2,1,0:T(8,128)(2,1)S(1)}, f32[32,1,128]{2,1,0:T(1,128)S(1)}) custom-call(s32[4,5]{1,0:T(4,128)S(1)} %copy-done.3, f32[256,256]{1,0:T(8,128)S(1)} %unit.1._, bf16[10,128,128]{2,1,0:T(8,128)(2,1)S(1)} %collective-permute-done.1.far, bf16[10,128,128]{2,1,0:T(8,128)(2,1)S(1)} %collective-permute-done.2.far_z, ...), custom_call_target="tpu_custom_call" | custom-call | flops 301989888 | bytes 4194304 | tf_op jit(solution)/shard_map/outer/pallas_call | solution.py:391
  11.6 0.0 copy-done.4
  11.6 0.0 copy-start.2
  11.6 0.6 %copy-done.2 = f32[32,1,128]{2,1,0:T(1,128)} copy-done((f32[32,1,128]{2,1,0:T(1,128)}, f32[32,1,128]{2,1,0:T(1,128)S(1)}, u32[]{:S(2)}) %copy-start.2) | copy-done | bytes 16408
  12.2 1.3 %collective-permute-start.4 = (bf16[2,256,256]{2,1,0:T(8,128)(2,1)}, bf16[2,256,256]{2,1,0:T(8,128)(2,1)}, u32[]{:S(2)}, u32[]{:S(2)}) collective-permute-start(bf16[2,256,256]{2,1,0:T(8,128)(2,1)} %get-tuple-element.39), channel_id=1, source_target_pairs={{1,2},{2,1},{3,4},{4,3},{5,6},{6,5},{7,8},{8,7},{9,10},{10,9},{11,... | collective-permute-start | bytes 786440 | tf_op jit(solution)/shard_map/ppermute | solution.py:597
  13.5 14.8 %all-to-all-start = ((f32[32,1,128]{2,1,0:T(1,128)}), f32[32,1,128]{2,1,0:T(1,128)S(1)}, u32[]{:S(2)}, u32[]{:S(2)}) async-start(f32[32,1,128]{2,1,0:T(1,128)} %copy-done.2), calls=%async_computation | async-start | bytes 32768 | tf_op jit(solution)/shard_map/all_to_all | solution.py:596
  28.4 0.0 copy-start.5
  28.4 0.7 %copy-done.5 = s32[4,5]{1,0:T(4,128)S(1)} copy-done((s32[4,5]{1,0:T(4,128)S(1)}, s32[4,5]{1,0:T(4,128)}, u32[]{:S(2)}) %copy-start.5) | copy-done | bytes 104
  29.1 2.2 %middle.1 = (bf16[4,5,128,128]{3,2,1,0:T(8,128)(2,1)}, bf16[10,256,256]{2,1,0:T(8,128)(2,1)S(1)}, f32[6,256,256]{2,1,0:T(8,128)S(1)}, bf16[5,256,256]{2,1,0:T(8,128)(2,1)S(1)}, s32[4,5]{1,0:T(4,128)S(1)}) custom-call(s32[4,5]{1,0:T(4,128)S(1)} %copy-done.5, ...), custom_call_target="tpu_custom_call", output_to_operand_aliasing={{1}: (1, {}), {2}: (2, {}), {3}: (3, {}), {4}: (0, {})} | custom-call | flops 301989888 | bytes 6291456 | tf_op jit(solution)/shard_map/middle/pallas_call | solution.py:454
  31.2 0.0 collective-permute-done.4.d_in
  31.2 2.9 %last.1 = (bf16[4,5,128,128]{3,2,1,0:T(8,128)(2,1)}, bf16[10,256,256]{2,1,0:T(8,128)(2,1)S(1)}, bf16[5,256,256]{2,1,0:T(8,128)(2,1)S(1)}, bf16[2,256,256]{2,1,0:T(8,128)(2,1)}, s32[4,5]{1,0:T(4,128)S(1)}) custom-call(s32[4,5]{1,0:T(4,128)S(1)} %get-tuple-element.36.pattern_in, ...), custom_call_target="tpu_custom_call", output_to_operand_aliasing={{0}: (4, {}), {1}: (1, {}), {2}: (2, {}), {3}: (3, {}), {4}... | custom-call | flops 704643072 | bytes 4194304 | tf_op jit(solution)/shard_map/last/pallas_call | solution.py:531
  34.1 1.4 %all-to-all-done.gathered = f32[32,1,128]{2,1,0:T(1,128)S(1)} async-done(((f32[32,1,128]{2,1,0:T(1,128)}), f32[32,1,128]{2,1,0:T(1,128)S(1)}, u32[]{:S(2)}, u32[]{:S(2)}) %all-to-all-start) | async-done | bytes 16416 | tf_op jit(solution)/shard_map/all_to_all | solution.py:596
  35.5 0.7 %norm.1 = f32[1,128]{1,0:T(1,128)} custom-call(f32[32,1,128]{2,1,0:T(1,128)S(1)} %all-to-all-done.gathered, bf16[10,256,256]{2,1,0:T(8,128)(2,1)S(1)} %get-tuple-element.43._), custom_call_target="tpu_custom_call" | custom-call | tf_op jit(solution)/shard_map/norm/pallas_call | solution.py:560
  (1 shorter events, 0.0 us)
Async XLA Ops:
  0.6 1.1 %copy-start = (bf16[4,5,128,128]{3,2,1,0:T(8,128)(2,1)S(1)}, bf16[4,5,128,128]{3,2,1,0:T(8,128)(2,1)}, u32[]{:S(2)}) copy-start(bf16[4,5,128,128]{3,2,1,0:T(8,128)(2,1)} %margin.1) | copy-start | bytes 1966084
  0.6 1.3 %copy-start.1 = (bf16[4,5,128,128]{3,2,1,0:T(8,128)(2,1)S(1)}, bf16[4,5,128,128]{3,2,1,0:T(8,128)(2,1)}, u32[]{:S(2)}) copy-start(bf16[4,5,128,128]{3,2,1,0:T(8,128)(2,1)} %factor.1) | copy-start | bytes 1966084
  0.6 1.3 %copy-start.3 = (s32[4,5]{1,0:T(4,128)S(1)}, s32[4,5]{1,0:T(4,128)}, u32[]{:S(2)}) copy-start(s32[4,5]{1,0:T(4,128)} %pattern.5) | copy-start | bytes 244
  2.9 2.8 %collective-permute-start = (bf16[31,128,128]{2,1,0:T(8,128)(2,1)S(1)}, bf16[31,128,128]{2,1,0:T(8,128)(2,1)S(1)}, u32[]{:S(2)}, u32[]{:S(2)}) collective-permute-start(bf16[31,128,128]{2,1,0:T(8,128)(2,1)S(1)} %get-tuple-element.23.near), channel_id=1, source_target_pairs={{0,1},{1,0},{2,3},{3,2},{4,5},{5,4},{6,7},{7,6},{8,9},{9,8},{10,11... | collective-permute-start | bytes 3047432 | tf_op jit(solution)/shard_map/ppermute | solution.py:589
  3.4 6.2 %collective-permute-start.1 = (bf16[10,128,128]{2,1,0:T(8,128)(2,1)S(1)}, bf16[10,128,128]{2,1,0:T(8,128)(2,1)S(1)}, u32[]{:S(2)}, u32[]{:S(2)}) collective-permute-start(bf16[10,128,128]{2,1,0:T(8,128)(2,1)S(1)} %get-tuple-element.24.far_s), channel_id=1, source_target_pairs={{1,2},{2,1},{3,4},{4,3},{5,6},{6,5},{9,10},{10,9},{11,12},{12,11},... | collective-permute-start | bytes 983048 | tf_op jit(solution)/shard_map/ppermute | solution.py:586
  4.1 5.5 %collective-permute-start.2 = (bf16[10,128,128]{2,1,0:T(8,128)(2,1)S(1)}, bf16[10,128,128]{2,1,0:T(8,128)(2,1)S(1)}, u32[]{:S(2)}, u32[]{:S(2)}) collective-permute-start(bf16[10,128,128]{2,1,0:T(8,128)(2,1)S(1)} %get-tuple-element.25.far_z), channel_id=1, source_target_pairs={{1,2},{2,1},{3,4},{4,3},{5,6},{6,5},{9,10},{10,9},{11,12},{12,11},... | collective-permute-start | bytes 983048 | tf_op jit(solution)/shard_map/ppermute | solution.py:587
  4.7 4.8 %collective-permute-start.3 = (bf16[2,2,128,128]{3,2,1,0:T(8,128)(2,1)S(1)}, bf16[2,2,128,128]{3,2,1,0:T(8,128)(2,1)S(1)}, u32[]{:S(2)}, u32[]{:S(2)}) collective-permute-start(bf16[2,2,128,128]{3,2,1,0:T(8,128)(2,1)S(1)} %get-tuple-element.29), channel_id=1, source_target_pairs={{7,8},{8,7},{15,16},{16,15},{23,24},{24,23}} | collective-permute-start | bytes 393224 | tf_op jit(solution)/shard_map/ppermute | solution.py:588
  9.5 2.1 %copy-start.4 = (s32[4,5]{1,0:T(4,128)}, s32[4,5]{1,0:T(4,128)S(1)}, u32[]{:S(2)}) copy-start(s32[4,5]{1,0:T(4,128)S(1)} %get-tuple-element.26.pattern_in) | copy-start | bytes 244
  11.6 0.6 %copy-start.2 = (f32[32,1,128]{2,1,0:T(1,128)}, f32[32,1,128]{2,1,0:T(1,128)S(1)}, u32[]{:S(2)}) copy-start(f32[32,1,128]{2,1,0:T(1,128)S(1)} %get-tuple-element.42) | copy-start | bytes 49156
  12.2 19.0 %collective-permute-start.4 = (bf16[2,256,256]{2,1,0:T(8,128)(2,1)}, bf16[2,256,256]{2,1,0:T(8,128)(2,1)}, u32[]{:S(2)}, u32[]{:S(2)}) collective-permute-start(bf16[2,256,256]{2,1,0:T(8,128)(2,1)} %get-tuple-element.39), channel_id=1, source_target_pairs={{1,2},{2,1},{3,4},{4,3},{5,6},{6,5},{7,8},{8,7},{9,10},{10,9},{11,... | collective-permute-start | bytes 786440 | tf_op jit(solution)/shard_map/ppermute | solution.py:597
  13.5 22.0 %all-to-all-start = ((f32[32,1,128]{2,1,0:T(1,128)}), f32[32,1,128]{2,1,0:T(1,128)S(1)}, u32[]{:S(2)}, u32[]{:S(2)}) async-start(f32[32,1,128]{2,1,0:T(1,128)} %copy-done.2), calls=%async_computation | async-start | bytes 32768 | tf_op jit(solution)/shard_map/all_to_all | solution.py:596
  28.4 0.7 %copy-start.5 = (s32[4,5]{1,0:T(4,128)S(1)}, s32[4,5]{1,0:T(4,128)}, u32[]{:S(2)}) copy-start(s32[4,5]{1,0:T(4,128)} %copy-done.4) | copy-start | bytes 244

commit v5 on v4

--- a/solution.py
+++ b/solution.py
@@ -552,7 +552,7 @@
 
 
 def norm_kernel(z, gathered, _, norm):
-    mean = jnp.sum(gathered[...]) * (1.0 / z.entries)
+    mean = jnp.sum(jnp.sum(gathered[...], axis=0)) * (1.0 / z.entries)
     norm[...] = jnp.sqrt(jnp.full(norm.shape, mean, jnp.float32))
 
 

time: 36.5 us -> 36.5 us (level)
  no operation moved by 1% of the time
where the time goes in v5:
time: 36.5 us; the launch traced here: 36.2 us
  starting transfers between devices  18.7 us (51%)
  Pallas kernels  12.6 us (35%)
  local copies, waits for them, and re-layouts  2.51 us (7%)
  waiting for transfers between devices  1.6 us (4%)
  between operations  0.8 us (2%)
    all_to_all x1, starting transfers between devices, per_device(): gathered = lax.all_to_all(spread, AXES, 0, 0, tiled=True)  14.8 us
    pallas_call x1, Pallas kernels, inner_step(): pl.pallas_call(functools.partial(inner_kernel, z), out_shape=(jax.ShapeDt...  3.89 us
    pallas_call x1, Pallas kernels, last_step(): pl.pallas_call(functools.partial(last_kernel, z), out_shape=tuple((jax.Sh...  2.88 us
    unnamed x12, local copies, waits for them, and re-layouts  2.51 us
    pallas_call x1, Pallas kernels, middle_step(): pl.pallas_call(functools.partial(middle_kernel, z), out_shape=(jax.ShapeD...  2.16 us
    pallas_call x1, Pallas kernels, outer_step(): pl.pallas_call(functools.partial(outer_kernel, z), out_shape=(z.tiles(2,...  2.01 us
    all_to_all x1, waiting for transfers between devices, per_device(): gathered = lax.all_to_all(spread, AXES, 0, 0, tiled=True)  1.39 us
    ppermute x1, starting transfers between devices, per_device(): d_in = lax.ppermute(d_out, AXES, swaps(far_pairs))  1.35 us
  transfers between devices with their start and end apart: 6, of which 2 were waited for; matrix products, arithmetic and copies ran while one was open for 0% of the time, Pallas kernels for 25%

profile of v5, /device:TPU:0, one launch (start us, length us, event | category | flops | bytes accessed | tf_op | source)
XLA Modules:
  0.0 36.2 jit_solution(1564785984927826778)
XLA Ops:
  0.6 0.0 copy-start
  0.6 0.0 copy-start.1
  0.6 0.0 copy-start.3
  0.7 1.0 %copy-done = bf16[4,5,128,128]{3,2,1,0:T(8,128)(2,1)S(1)} copy-done((bf16[4,5,128,128]{3,2,1,0:T(8,128)(2,1)S(1)}, bf16[4,5,128,128]{3,2,1,0:T(8,128)(2,1)}, u32[]{:S(2)}) %copy-start) | copy-done | bytes 655384
  1.7 0.2 copy-done.1
  1.9 0.0 copy-done.3
  1.9 0.9 %pack.1 = (bf16[31,128,128]{2,1,0:T(8,128)(2,1)S(1)}, bf16[10,128,128]{2,1,0:T(8,128)(2,1)S(1)}, bf16[10,128,128]{2,1,0:T(8,128)(2,1)S(1)}, bf16[2,2,128,128]{3,2,1,0:T(8,128)(2,1)S(1)}) custom-call(bf16[4,5,128,128]{3,2,1,0:T(8,128)(2,1)S(1)} %copy-done, bf16[4,5,128,128]{3,2,1,0:T(8,128)(2,1)S(1)} %copy-done.1, s32[4,5]{1,0:T(4,128)S(1)} %copy-done.3, ...), custom_call_target="tpu_custom_call" | custom-call | tf_op jit(solution)/shard_map/pack/pallas_call | solution.py:194
  2.9 0.5 %collective-permute-start = (bf16[31,128,128]{2,1,0:T(8,128)(2,1)S(1)}, bf16[31,128,128]{2,1,0:T(8,128)(2,1)S(1)}, u32[]{:S(2)}, u32[]{:S(2)}) collective-permute-start(bf16[31,128,128]{2,1,0:T(8,128)(2,1)S(1)} %get-tuple-element.23.near), channel_id=1, source_target_pairs={{0,1},{1,0},{2,3},{3,2},{4,5},{5,4},{6,7},{7,6},{8,9},{9,8},{10,11... | collective-permute-start | bytes 3047432 | tf_op jit(solution)/shard_map/ppermute | solution.py:589
  3.4 0.7 %collective-permute-start.1 = (bf16[10,128,128]{2,1,0:T(8,128)(2,1)S(1)}, bf16[10,128,128]{2,1,0:T(8,128)(2,1)S(1)}, u32[]{:S(2)}, u32[]{:S(2)}) collective-permute-start(bf16[10,128,128]{2,1,0:T(8,128)(2,1)S(1)} %get-tuple-element.24.far_s), channel_id=1, source_target_pairs={{1,2},{2,1},{3,4},{4,3},{5,6},{6,5},{9,10},{10,9},{11,12},{12,11},... | collective-permute-start | bytes 983048 | tf_op jit(solution)/shard_map/ppermute | solution.py:586
  4.1 0.7 %collective-permute-start.2 = (bf16[10,128,128]{2,1,0:T(8,128)(2,1)S(1)}, bf16[10,128,128]{2,1,0:T(8,128)(2,1)S(1)}, u32[]{:S(2)}, u32[]{:S(2)}) collective-permute-start(bf16[10,128,128]{2,1,0:T(8,128)(2,1)S(1)} %get-tuple-element.25.far_z), channel_id=1, source_target_pairs={{1,2},{2,1},{3,4},{4,3},{5,6},{6,5},{9,10},{10,9},{11,12},{12,11},... | collective-permute-start | bytes 983048 | tf_op jit(solution)/shard_map/ppermute | solution.py:587
  4.7 0.7 %collective-permute-start.3 = (bf16[2,2,128,128]{3,2,1,0:T(8,128)(2,1)S(1)}, bf16[2,2,128,128]{3,2,1,0:T(8,128)(2,1)S(1)}, u32[]{:S(2)}, u32[]{:S(2)}) collective-permute-start(bf16[2,2,128,128]{3,2,1,0:T(8,128)(2,1)S(1)} %get-tuple-element.29), channel_id=1, source_target_pairs={{7,8},{8,7},{15,16},{16,15},{23,24},{24,23}} | collective-permute-start | bytes 393224 | tf_op jit(solution)/shard_map/ppermute | solution.py:588
  5.4 0.2 collective-permute-done.beside
  5.6 3.9 %inner.1 = (bf16[3,3,256,256]{3,2,1,0:T(8,128)(2,1)S(1)}, bf16[3,256,256]{2,1,0:T(8,128)(2,1)S(1)}, f32[2,256,256]{2,1,0:T(8,128)S(1)}, f32[2,256,256]{2,1,0:T(8...) custom-call(s32[4,5]{1,0:T(4,128)S(1)} %copy-done.3, ...), custom_call_target="tpu_custom_call" | custom-call | flops 1811939328 | bytes 8388608 | tf_op jit(solution)/shard_map/inner/pallas_call | solution.py:313
  9.5 0.0 copy-start.4
  9.5 0.0 collective-permute-done.3.cross
  9.5 0.0 collective-permute-done.1.far
  9.5 0.0 collective-permute-done.2.far_z
  9.6 2.0 %outer.1 = (bf16[2,256,256]{2,1,0:T(8,128)(2,1)}, bf16[5,256,256]{2,1,0:T(8,128)(2,1)S(1)}, f32[32,1,128]{2,1,0:T(1,128)S(1)}) custom-call(s32[4,5]{1,0:T(4,128)S(1)} %copy-done.3, f32[256,256]{1,0:T(8,128)S(1)} %unit.1._, bf16[10,128,128]{2,1,0:T(8,128)(2,1)S(1)} %collective-permute-done.1.far, bf16[10,128,128]{2,1,0:T(8,128)(2,1)S(1)} %collective-permute-done.2.far_z, ...), custom_call_target="tpu_custom_call" | custom-call | flops 301989888 | bytes 4194304 | tf_op jit(solution)/shard_map/outer/pallas_call | solution.py:391
  11.6 0.0 copy-done.4
  11.6 0.0 copy-start.2
  11.6 0.6 %copy-done.2 = f32[32,1,128]{2,1,0:T(1,128)} copy-done((f32[32,1,128]{2,1,0:T(1,128)}, f32[32,1,128]{2,1,0:T(1,128)S(1)}, u32[]{:S(2)}) %copy-start.2) | copy-done | bytes 16408
  12.2 1.3 %collective-permute-start.4 = (bf16[2,256,256]{2,1,0:T(8,128)(2,1)}, bf16[2,256,256]{2,1,0:T(8,128)(2,1)}, u32[]{:S(2)}, u32[]{:S(2)}) collective-permute-start(bf16[2,256,256]{2,1,0:T(8,128)(2,1)} %get-tuple-element.39), channel_id=1, source_target_pairs={{1,2},{2,1},{3,4},{4,3},{5,6},{6,5},{7,8},{8,7},{9,10},{10,9},{11,... | collective-permute-start | bytes 786440 | tf_op jit(solution)/shard_map/ppermute | solution.py:597
  13.5 14.8 %all-to-all-start = ((f32[32,1,128]{2,1,0:T(1,128)}), f32[32,1,128]{2,1,0:T(1,128)S(1)}, u32[]{:S(2)}, u32[]{:S(2)}) async-start(f32[32,1,128]{2,1,0:T(1,128)} %copy-done.2), calls=%async_computation | async-start | bytes 32768 | tf_op jit(solution)/shard_map/all_to_all | solution.py:596
  28.4 0.0 copy-start.5
  28.4 0.7 %copy-done.5 = s32[4,5]{1,0:T(4,128)S(1)} copy-done((s32[4,5]{1,0:T(4,128)S(1)}, s32[4,5]{1,0:T(4,128)}, u32[]{:S(2)}) %copy-start.5) | copy-done | bytes 104
  29.1 2.2 %middle.1 = (bf16[4,5,128,128]{3,2,1,0:T(8,128)(2,1)}, bf16[10,256,256]{2,1,0:T(8,128)(2,1)S(1)}, f32[6,256,256]{2,1,0:T(8,128)S(1)}, bf16[5,256,256]{2,1,0:T(8,128)(2,1)S(1)}, s32[4,5]{1,0:T(4,128)S(1)}) custom-call(s32[4,5]{1,0:T(4,128)S(1)} %copy-done.5, ...), custom_call_target="tpu_custom_call", output_to_operand_aliasing={{1}: (1, {}), {2}: (2, {}), {3}: (3, {}), {4}: (0, {})} | custom-call | flops 301989888 | bytes 6291456 | tf_op jit(solution)/shard_map/middle/pallas_call | solution.py:454
  31.2 0.0 collective-permute-done.4.d_in
  31.2 2.9 %last.1 = (bf16[4,5,128,128]{3,2,1,0:T(8,128)(2,1)}, bf16[10,256,256]{2,1,0:T(8,128)(2,1)S(1)}, bf16[5,256,256]{2,1,0:T(8,128)(2,1)S(1)}, bf16[2,256,256]{2,1,0:T(8,128)(2,1)}, s32[4,5]{1,0:T(4,128)S(1)}) custom-call(s32[4,5]{1,0:T(4,128)S(1)} %get-tuple-element.36.pattern_in, ...), custom_call_target="tpu_custom_call", output_to_operand_aliasing={{0}: (4, {}), {1}: (1, {}), {2}: (2, {}), {3}: (3, {}), {4}... | custom-call | flops 704643072 | bytes 4194304 | tf_op jit(solution)/shard_map/last/pallas_call | solution.py:531
  34.1 1.4 %all-to-all-done.gathered = f32[32,1,128]{2,1,0:T(1,128)S(1)} async-done(((f32[32,1,128]{2,1,0:T(1,128)}), f32[32,1,128]{2,1,0:T(1,128)S(1)}, u32[]{:S(2)}, u32[]{:S(2)}) %all-to-all-start) | async-done | bytes 16416 | tf_op jit(solution)/shard_map/all_to_all | solution.py:596
  35.5 0.7 %norm.1 = f32[1,128]{1,0:T(1,128)} custom-call(f32[32,1,128]{2,1,0:T(1,128)S(1)} %all-to-all-done.gathered, bf16[10,256,256]{2,1,0:T(8,128)(2,1)S(1)} %get-tuple-element.43._), custom_call_target="tpu_custom_call" | custom-call | tf_op jit(solution)/shard_map/norm/pallas_call | solution.py:560
  (1 shorter events, 0.0 us)
Async XLA Ops:
  0.6 1.1 %copy-start = (bf16[4,5,128,128]{3,2,1,0:T(8,128)(2,1)S(1)}, bf16[4,5,128,128]{3,2,1,0:T(8,128)(2,1)}, u32[]{:S(2)}) copy-start(bf16[4,5,128,128]{3,2,1,0:T(8,128)(2,1)} %margin.1) | copy-start | bytes 1966084
  0.6 1.3 %copy-start.1 = (bf16[4,5,128,128]{3,2,1,0:T(8,128)(2,1)S(1)}, bf16[4,5,128,128]{3,2,1,0:T(8,128)(2,1)}, u32[]{:S(2)}) copy-start(bf16[4,5,128,128]{3,2,1,0:T(8,128)(2,1)} %factor.1) | copy-start | bytes 1966084
  0.6 1.3 %copy-start.3 = (s32[4,5]{1,0:T(4,128)S(1)}, s32[4,5]{1,0:T(4,128)}, u32[]{:S(2)}) copy-start(s32[4,5]{1,0:T(4,128)} %pattern.5) | copy-start | bytes 244
  2.9 2.8 %collective-permute-start = (bf16[31,128,128]{2,1,0:T(8,128)(2,1)S(1)}, bf16[31,128,128]{2,1,0:T(8,128)(2,1)S(1)}, u32[]{:S(2)}, u32[]{:S(2)}) collective-permute-start(bf16[31,128,128]{2,1,0:T(8,128)(2,1)S(1)} %get-tuple-element.23.near), channel_id=1, source_target_pairs={{0,1},{1,0},{2,3},{3,2},{4,5},{5,4},{6,7},{7,6},{8,9},{9,8},{10,11... | collective-permute-start | bytes 3047432 | tf_op jit(solution)/shard_map/ppermute | solution.py:589
  3.4 6.2 %collective-permute-start.1 = (bf16[10,128,128]{2,1,0:T(8,128)(2,1)S(1)}, bf16[10,128,128]{2,1,0:T(8,128)(2,1)S(1)}, u32[]{:S(2)}, u32[]{:S(2)}) collective-permute-start(bf16[10,128,128]{2,1,0:T(8,128)(2,1)S(1)} %get-tuple-element.24.far_s), channel_id=1, source_target_pairs={{1,2},{2,1},{3,4},{4,3},{5,6},{6,5},{9,10},{10,9},{11,12},{12,11},... | collective-permute-start | bytes 983048 | tf_op jit(solution)/shard_map/ppermute | solution.py:586
  4.1 5.5 %collective-permute-start.2 = (bf16[10,128,128]{2,1,0:T(8,128)(2,1)S(1)}, bf16[10,128,128]{2,1,0:T(8,128)(2,1)S(1)}, u32[]{:S(2)}, u32[]{:S(2)}) collective-permute-start(bf16[10,128,128]{2,1,0:T(8,128)(2,1)S(1)} %get-tuple-element.25.far_z), channel_id=1, source_target_pairs={{1,2},{2,1},{3,4},{4,3},{5,6},{6,5},{9,10},{10,9},{11,12},{12,11},... | collective-permute-start | bytes 983048 | tf_op jit(solution)/shard_map/ppermute | solution.py:587
  4.7 4.8 %collective-permute-start.3 = (bf16[2,2,128,128]{3,2,1,0:T(8,128)(2,1)S(1)}, bf16[2,2,128,128]{3,2,1,0:T(8,128)(2,1)S(1)}, u32[]{:S(2)}, u32[]{:S(2)}) collective-permute-start(bf16[2,2,128,128]{3,2,1,0:T(8,128)(2,1)S(1)} %get-tuple-element.29), channel_id=1, source_target_pairs={{7,8},{8,7},{15,16},{16,15},{23,24},{24,23}} | collective-permute-start | bytes 393224 | tf_op jit(solution)/shard_map/ppermute | solution.py:588
  9.5 2.1 %copy-start.4 = (s32[4,5]{1,0:T(4,128)}, s32[4,5]{1,0:T(4,128)S(1)}, u32[]{:S(2)}) copy-start(s32[4,5]{1,0:T(4,128)S(1)} %get-tuple-element.26.pattern_in) | copy-start | bytes 244
  11.6 0.6 %copy-start.2 = (f32[32,1,128]{2,1,0:T(1,128)}, f32[32,1,128]{2,1,0:T(1,128)S(1)}, u32[]{:S(2)}) copy-start(f32[32,1,128]{2,1,0:T(1,128)S(1)} %get-tuple-element.42) | copy-start | bytes 49156
  12.2 19.0 %collective-permute-start.4 = (bf16[2,256,256]{2,1,0:T(8,128)(2,1)}, bf16[2,256,256]{2,1,0:T(8,128)(2,1)}, u32[]{:S(2)}, u32[]{:S(2)}) collective-permute-start(bf16[2,256,256]{2,1,0:T(8,128)(2,1)} %get-tuple-element.39), channel_id=1, source_target_pairs={{1,2},{2,1},{3,4},{4,3},{5,6},{6,5},{7,8},{8,7},{9,10},{10,9},{11,... | collective-permute-start | bytes 786440 | tf_op jit(solution)/shard_map/ppermute | solution.py:597
  13.5 22.0 %all-to-all-start = ((f32[32,1,128]{2,1,0:T(1,128)}), f32[32,1,128]{2,1,0:T(1,128)S(1)}, u32[]{:S(2)}, u32[]{:S(2)}) async-start(f32[32,1,128]{2,1,0:T(1,128)} %copy-done.2), calls=%async_computation | async-start | bytes 32768 | tf_op jit(solution)/shard_map/all_to_all | solution.py:596
  28.4 0.7 %copy-start.5 = (s32[4,5]{1,0:T(4,128)S(1)}, s32[4,5]{1,0:T(4,128)}, u32[]{:S(2)}) copy-start(s32[4,5]{1,0:T(4,128)} %copy-done.4) | copy-start | bytes 244
